TPU v7x, 128 devices: a whole 4x4x4 slice. The times are simulated.
128 devices in a mesh: obs: 8 (over z, core), src: 16 (over y, x).
Axes of the slice: x: 4, y: 4, z: 4, core: 2. Of those that a mesh axis runs over, the one named last changes fastest.
Arguments:
- history: bfloat16 [3, 256, 64, 1536], P(None, ('obs', 'src')), may hold values from -6 to 6
- incident: bfloat16 [5, 256, 64, 1536], P(None, ('obs', 'src')), may hold values from -6 to 6
- proj_basis: bfloat16 [256, 64, 1536], P(('obs', 'src')), may hold values from -0.15625 to 0.15625
- expand_basis: bfloat16 [256, 64, 1536], P(('obs', 'src')), may hold values from -0.75 to 0.75
- near_inverse: bfloat16 [256, 1536, 1536], P(('obs', 'src')), may hold values from -0.15625 to 0.15625
- couplings: bfloat16 [2, 16384, 8, 16, 128], P(None, 'obs', None, 'src'), may hold values from -0.046875 to 0.046875
- lags: int32 [256, 8, 16, 2], P('obs', None, 'src'), may hold values from 0 to 2, as said below
Outputs:
- currents: bfloat16 [5, 256, 64, 1536], P(None, ('obs', 'src'))
Inputs may be any that keep to these rules, and one draw needn't show every extreme that they name: lags[j, o, s, k] is the lag from source cluster j to observer cluster (o * 16 + s) * 2 + k. Entries are 0, 1 or 2, and the entry of every cluster with itself is 0.
All inputs are finite; a program needn't handle non-finite values.
Results may differ from a plain program's by a relative error of at most 0.025.
Values may be sent and summed in bfloat16 or wider, within the bound.
No kernel may reach another device: no remote copies, remote signals or barrier semaphores. Data moves between devices by JAX's collectives and lax.ppermute only.
A program may use at most 192 MiB of HBM per device.

v0:
```python
import jax
import jax.numpy as jnp
from jax import lax
from jax.sharding import PartitionSpec as P

STEPS = 5
TAPS = 2
HIST = 3


def per_device(history, incident, proj_basis, expand_basis, near_inverse, couplings, lags):
    rank = proj_basis.shape[1]
    local_clusters = proj_basis.shape[0]
    excite = history.shape[2]
    src_rows = couplings.shape[1]
    obs_cols = couplings.shape[2] * couplings.shape[3] * couplings.shape[4]
    src_clusters = lags.shape[0]
    obs_clusters = lags.shape[1] * lags.shape[2] * lags.shape[3]
    kernel = couplings.reshape(TAPS, src_clusters, rank, obs_clusters, rank)
    lag_pairs = lags.reshape(src_clusters, obs_clusters)
    matrices = []
    for delay in range(1, HIST + 1):
        combined = jnp.zeros_like(kernel[0])
        for tap_index in range(TAPS):
            if delay - tap_index >= 1:
                chosen = (lag_pairs == delay - tap_index)[:, None, :, None]
                combined = jnp.where(chosen, kernel[tap_index], combined)
        matrices.append(combined.reshape(src_rows, obs_cols))

    def project(current):
        projected = jnp.einsum(
            "ceb,crb->ecr", current, proj_basis, preferred_element_type=jnp.float32
        )
        return projected.astype(jnp.bfloat16).reshape(excite, local_clusters * rank)

    def couple(columns, delay):
        return jnp.dot(columns, matrices[delay - 1], preferred_element_type=jnp.float32)

    stacked = jnp.stack([project(history[slot_index]) for slot_index in range(HIST)])
    gathered = lax.all_gather(stacked, "src", axis=2, tiled=True)
    past = [gathered[slot_index] for slot_index in range(HIST)]
    results = []
    latest = None
    for step in range(STEPS):
        if step > 0:
            newest = lax.all_gather(latest, "src", axis=1, tiled=True)
            past = past[1:] + [newest]
        partial_value = couple(past[-1], 1) + couple(past[-2], 2) + couple(past[-3], 3)
        field = lax.psum_scatter(
            partial_value.astype(jnp.bfloat16), "obs", scatter_dimension=1, tiled=True
        )
        field_cast = field.reshape(excite, local_clusters, rank)
        far_field = jnp.einsum(
            "ecr,crb->ceb", field_cast, expand_basis, preferred_element_type=jnp.float32
        )
        residual_field = (incident[step].astype(jnp.float32) - far_field).astype(jnp.bfloat16)
        current = jnp.einsum(
            "ceb,cbd->ced", residual_field, near_inverse, preferred_element_type=jnp.float32
        ).astype(jnp.bfloat16)
        results.append(current)
        if step + 1 < STEPS:
            latest = project(current)
    return jnp.stack(results)


def solution(mesh):
    placed = (
        P(None, ("obs", "src"), None, None),
        P(None, ("obs", "src"), None, None),
        P(("obs", "src"), None, None),
        P(("obs", "src"), None, None),
        P(("obs", "src"), None, None),
        P(None, "obs", None, "src", None),
        P("obs", None, "src", None),
    )
    return jax.shard_map(
        per_device,
        mesh=mesh,
        in_specs=placed,
        out_specs=P(None, ("obs", "src"), None, None),
        check_vma=False,
    )
```

profile of v0, /device:TPU:0, one launch (start us, length us, event | category | flops | bytes accessed | tf_op | source)
XLA Modules:
  0.0 448.4 jit_solution(8503899855921014617)
XLA Ops:
  6.5 1.4 convolution_convert_fusion.11
  8.0 1.4 convolution_convert_fusion.10
  9.3 1.4 convolution_convert_fusion.9
  10.7 0.7 broadcast_compare_fusion
  11.8 5.7 %fusion.42 = (bf16[1,2048,8,1,128]{4,2,3,1,0:T(8,128)(2,1)}, bf16[1,2048,8,1,128]{4,2,3,1,0:T(8,128)(2,1)}) fusion(bf16[2,2048,8,1,128]{4,2,3,1,0:T(8,128)(2,1)} %param.12), kind=kLoop, calls=%fused_computation.88 | loop fusion | bytes 16777216 | tf_op jit(solution)/shard_map/slice | solution.py:27
  17.5 11.1 %squeeze.40 = bf16[32,64,16,64]{3,2,1,0:T(8,128)(2,1)} reshape(bf16[1,2048,8,1,128]{4,2,3,1,0:T(8,128)(2,1)} %get-tuple-element.9) | data formatting | bytes 8388608 | tf_op jit(solution)/shard_map/squeeze | solution.py:27
  28.6 11.1 %squeeze.42 = bf16[32,64,16,64]{3,2,1,0:T(8,128)(2,1)} reshape(bf16[1,2048,8,1,128]{4,2,3,1,0:T(8,128)(2,1)} %get-tuple-element.8) | data formatting | bytes 8388608 | tf_op jit(solution)/shard_map/squeeze | solution.py:27
  39.7 15.2 %select_select_fusion = (bf16[32,64,16,64]{3,2,1,0:T(8,128)(2,1)}, bf16[32,64,16,64]{3,2,1,0:T(8,128)(2,1)}, bf16[32,64,16,64]{3,2,1,0:T(8,128)(2,1)}) fusion(bf16[32,64,16,64]{3,2,1,0:T(8,128)(2,1)} %squeeze.42, bf16[32,64,16,64]{3,2,1,0:T(8,128)(2,1)} %squeeze.40, pred[32,16]{1,0:T(8,128)(4,1)S(1)} %copy.20, pred[32,16]{1,0:T(8,128)(4,1)S(1)} %copy.19, ...), kind=kLoop, calls=%fused_computation | loop fusion | flops 10485760 | bytes 20973056 | tf_op jit(solution)/shard_map/jit(_where)/select_n | solution.py:27
  54.8 11.9 %select_n.97 = bf16[2048,1024]{1,0:T(8,128)(2,1)} reshape(bf16[32,64,16,64]{3,2,1,0:T(8,128)(2,1)} %get-tuple-element.7) | data formatting | bytes 8388608 | tf_op jit(solution)/shard_map/jit(_where)/select_n | solution.py:27
  66.7 26.3 %all_gather.15 = bf16[3,64,2048]{1,2,0:T(8,128)(2,1)S(1)} all-gather(bf16[3,64,128]{1,2,0:T(8,128)(2,1)S(1)} %pad_maximum_fusion), channel_id=1, replica_groups=mesh['obs'=8,'src'=16] {'src'}, dimensions={2}, use_global_device_ids=true | all-gather | bytes 835584 | tf_op jit(solution)/shard_map/all_gather | solution.py:40
  93.1 11.9 %select_n.100 = bf16[2048,1024]{1,0:T(8,128)(2,1)} reshape(bf16[32,64,16,64]{3,2,1,0:T(8,128)(2,1)} %get-tuple-element.6) | data formatting | bytes 8388608 | tf_op jit(solution)/shard_map/jit(_where)/select_n | solution.py:27
  104.9 11.9 %select_n.103 = bf16[2048,1024]{1,0:T(8,128)(2,1)} reshape(bf16[32,64,16,64]{3,2,1,0:T(8,128)(2,1)} %get-tuple-element.5) | data formatting | bytes 8388608 | tf_op jit(solution)/shard_map/jit(_where)/select_n | solution.py:27
  116.8 3.2 fusion.21
  120.0 3.1 convolution_add_fusion.9
  123.1 0.9 fusion.7
  124.0 0.8 copy.30
  124.9 0.3 reduce-scatter.18.cloned.1.call-start
  125.2 3.1 broadcast_in_dim.35
  128.3 11.8 %broadcast_in_dim.38 = pred[2048,1024]{1,0:T(32,128)(4,1)} reshape(pred[32,64,16,64]{3,2,1,0:T(8,128)(4,1)} %broadcast_in_dim.35) | data formatting | bytes 4194304 | tf_op jit(solution)/shard_map/jit(_where)/broadcast_in_dim | solution.py:27
  140.1 3.1 broadcast_in_dim.36
  143.2 11.8 %broadcast_in_dim.39 = pred[2048,1024]{1,0:T(32,128)(4,1)} reshape(pred[32,64,16,64]{3,2,1,0:T(8,128)(4,1)} %broadcast_in_dim.36) | data formatting | bytes 4194304 | tf_op jit(solution)/shard_map/jit(_where)/broadcast_in_dim | solution.py:27
  154.9 0.9 reduce-scatter.16.cloned.1.call-done
  155.9 6.6 %bitcast_dynamic-update-slice_fusion.3 = (bf16[5,2,64,1536]{3,2,1,0:T(8,128)(2,1)}, bf16[2,64,1536]{2,1,0:T(8,128)(2,1)S(1)}) fusion(bf16[2,1536,1536]{2,1,0:T(8,128)(2,1)} %param.11, bf16[64,2,64]{0,2,1:T(8,128)(2,1)} %bitcast.218, bf16[2,64,1536]{2,1,0:T(8,128)(2,1)S(1)} %copy-done, bf16[5,2,64,1536]{3,2,1,0:T(8,128)(2,1)} %param.8), kind=kOutput, calls=%fused_computation.68 | convolution fusion | flops 629932032 | bytes 11042816 | tf_op jit(solution)/shard_map/ceb,cbd->ced/dot_general | solution.py:57
  162.5 0.2 fusion.12
  162.9 24.0 %all_gather.16 = bf16[64,2048]{1,0:T(8,128)(2,1)S(1)} all-gather(bf16[64,128]{1,0:T(8,128)(2,1)S(1)} %reshape.176), channel_id=1, replica_groups=mesh['obs'=8,'src'=16] {'src'}, dimensions={1}, use_global_device_ids=true | all-gather | bytes 278528 | tf_op jit(solution)/shard_map/all_gather | solution.py:46
  186.8 4.7 %fusion.41 = f32[64,1024]{1,0:T(8,128)S(1)} fusion(bf16[64,2048]{1,0:T(8,128)(2,1)S(1)} %all_gather.16, pred[2048,1024]{1,0:T(32,128)(4,1)} %broadcast_in_dim.38, bf16[256,8,8,128]{3,2,1,0:T(8,128)(2,1)} %bitcast.206), kind=kOutput, calls=%fused_computation.87 | convolution fusion | flops 270532608 | bytes 6815744 | tf_op jit(solution)/shard_map/dot_general | solution.py:37
  191.6 0.9 convolution_add_fusion.7
  192.5 1.3 copy-done.2
  193.7 0.9 fusion.8
  194.6 0.9 copy.32
  195.5 0.6 reduce-scatter.20.cloned.1.call-start
  196.1 7.3 %bitcast_select_fusion.1 = bf16[2048,1024]{1,0:T(8,128)(2,1)} fusion(pred[2048,1024]{1,0:T(32,128)(4,1)} %broadcast_in_dim.38, pred[2048,1024]{1,0:T(32,128)(4,1)} %broadcast_in_dim.39, bf16[256,8,8,128]{3,2,1,0:T(8,128)(2,1)} %bitcast.203, bf16[256,8,8,128]{3,2,1,0:T(8,128)(2,1)} %bitcast.207), kind=kLoop, calls=%fused_computation.4 | loop fusion | flops 4194304 | bytes 16777216 | tf_op jit(solution)/shard_map/jit(_where)/select_n | solution.py:27
  203.4 20.7 %reduce-scatter.18.cloned.1.call-done = bf16[128,64]{1,0:T(8,128)(2,1)} async-done(((bf16[1024,64]{1,0:T(8,128)(2,1)}), bf16[128,64]{1,0:T(8,128)(2,1)}) %reduce-scatter.18.cloned.1.call-update) | async-done | bytes 16400
  224.1 6.6 %bitcast_dynamic-update-slice_fusion.2 = (bf16[5,2,64,1536]{3,2,1,0:T(8,128)(2,1)}, bf16[2,64,1536]{2,1,0:T(8,128)(2,1)S(1)}) fusion(bf16[5,2,64,1536]{3,2,1,0:T(8,128)(2,1)} %get-tuple-element.13, bf16[2,1536,1536]{2,1,0:T(8,128)(2,1)} %param.11, bf16[64,2,64]{0,2,1:T(8,128)(2,1)} %bitcast.220, bf16[2,64,1536]{2,1,0:T(8,128)(2,1)S(1)} %copy-done, ...), kind=kOutput, calls=%fused_computation.67 | convolution fusion | flops 629932032 | bytes 11042816 | tf_op jit(solution)/shard_map/ceb,cbd->ced/dot_general | solution.py:57
  230.7 0.2 fusion.13
  231.1 24.0 %all_gather.17 = bf16[64,2048]{1,0:T(8,128)(2,1)S(1)} all-gather(bf16[64,128]{1,0:T(8,128)(2,1)S(1)} %reshape.178), channel_id=1, replica_groups=mesh['obs'=8,'src'=16] {'src'}, dimensions={1}, use_global_device_ids=true | all-gather | bytes 278528 | tf_op jit(solution)/shard_map/all_gather | solution.py:46
  255.1 4.7 %fusion.40 = f32[64,1024]{1,0:T(8,128)S(1)} fusion(bf16[64,2048]{1,0:T(8,128)(2,1)S(1)} %all_gather.17, pred[2048,1024]{1,0:T(32,128)(4,1)} %broadcast_in_dim.38, bf16[256,8,8,128]{3,2,1,0:T(8,128)(2,1)} %bitcast.208), kind=kOutput, calls=%fused_computation.86 | convolution fusion | flops 270532608 | bytes 6815744 | tf_op jit(solution)/shard_map/dot_general | solution.py:37
  259.8 0.9 convolution_add_fusion.5
  260.7 1.3 copy-done.3
  262.0 0.9 fusion.9
  262.9 0.8 copy.34
  263.8 3.2 broadcast_in_dim.37
  267.0 11.8 %broadcast_in_dim.40 = pred[2048,1024]{1,0:T(32,128)(4,1)} reshape(pred[32,64,16,64]{3,2,1,0:T(8,128)(4,1)} %broadcast_in_dim.37) | data formatting | bytes 4194304 | tf_op jit(solution)/shard_map/jit(_where)/broadcast_in_dim | solution.py:27
  278.8 12.7 %reduce-scatter.20.cloned.1.call-done = bf16[128,64]{1,0:T(8,128)(2,1)} async-done(((bf16[1024,64]{1,0:T(8,128)(2,1)}), bf16[128,64]{1,0:T(8,128)(2,1)}) %reduce-scatter.20.cloned.1.call-update) | async-done | bytes 16400
  291.5 6.6 %bitcast_dynamic-update-slice_fusion.1 = (bf16[5,2,64,1536]{3,2,1,0:T(8,128)(2,1)}, bf16[2,64,1536]{2,1,0:T(8,128)(2,1)S(1)}) fusion(bf16[5,2,64,1536]{3,2,1,0:T(8,128)(2,1)} %get-tuple-element.15, bf16[2,1536,1536]{2,1,0:T(8,128)(2,1)} %param.11, bf16[64,2,64]{0,2,1:T(8,128)(2,1)} %bitcast.219, bf16[2,64,1536]{2,1,0:T(8,128)(2,1)S(1)} %copy-done, ...), kind=kOutput, calls=%fused_computation.66 | convolution fusion | flops 629932032 | bytes 11042816 | tf_op jit(solution)/shard_map/ceb,cbd->ced/dot_general | solution.py:57
  298.0 0.2 fusion.14
  298.4 24.3 %all_gather.18 = bf16[64,2048]{1,0:T(8,128)(2,1)S(1)} all-gather(bf16[64,128]{1,0:T(8,128)(2,1)S(1)} %reshape.180), channel_id=1, replica_groups=mesh['obs'=8,'src'=16] {'src'}, dimensions={1}, use_global_device_ids=true | all-gather | bytes 278528 | tf_op jit(solution)/shard_map/all_gather | solution.py:46
  322.7 0.7 copy-done.16
  323.4 4.7 %fusion.39 = f32[64,1024]{1,0:T(8,128)S(1)} fusion(bf16[64,2048]{1,0:T(8,128)(2,1)S(1)} %all_gather.18, pred[2048,1024]{1,0:T(32,128)(4,1)} %broadcast_in_dim.38, bf16[256,8,8,128]{3,2,1,0:T(8,128)(2,1)} %bitcast.209), kind=kOutput, calls=%fused_computation.85 | convolution fusion | flops 270532608 | bytes 6815744 | tf_op jit(solution)/shard_map/dot_general | solution.py:37
  328.1 0.9 convolution_add_fusion.3
  329.0 1.4 copy-done.8
  330.5 4.7 %fusion.10 = bf16[64,1024]{1,0:T(8,128)(2,1)S(1)} fusion(f32[64,1024]{1,0:T(8,128)S(1)} %convolution_add_fusion.3, bf16[64,2048]{1,0:T(8,128)(2,1)S(1)} %copy-done.15, pred[2048,1024]{1,0:T(32,128)(4,1)S(1)} %copy-done.12, pred[2048,1024]{1,0:T(32,128)(4,1)} %broadcast_in_dim.40, bf16[256,8,8,128]{3,2,1,0:T(8,128)(2,1)S(1)} %bitcast.204, ...), kind=kOutput, calls=%fused_computation.38 | convolution fusion | flops 272760832 | bytes 13238272 | tf_op jit(solution)/shard_map/dot_general | solution.py:37
  335.1 0.8 copy.36
  336.0 27.6 %reduce-scatter.22.cloned.1.call-done = bf16[128,64]{1,0:T(8,128)(2,1)} async-done(((bf16[1024,64]{1,0:T(8,128)(2,1)}), bf16[128,64]{1,0:T(8,128)(2,1)}) %reduce-scatter.22.cloned.1.call-update) | async-done | bytes 16400
  363.7 6.6 %bitcast_dynamic-update-slice_fusion = (bf16[5,2,64,1536]{3,2,1,0:T(8,128)(2,1)}, bf16[2,64,1536]{2,1,0:T(8,128)(2,1)S(1)}) fusion(bf16[5,2,64,1536]{3,2,1,0:T(8,128)(2,1)} %get-tuple-element.17, bf16[2,1536,1536]{2,1,0:T(8,128)(2,1)} %param.11, bf16[64,2,64]{0,2,1:T(8,128)(2,1)} %bitcast.221, bf16[2,64,1536]{2,1,0:T(8,128)(2,1)S(1)} %copy-done, ...), kind=kOutput, calls=%fused_computation.65 | convolution fusion | flops 629932032 | bytes 11042816 | tf_op jit(solution)/shard_map/ceb,cbd->ced/dot_general | solution.py:57
  370.2 0.2 fusion.15
  370.6 24.2 %all_gather.19 = bf16[64,2048]{1,0:T(8,128)(2,1)S(1)} all-gather(bf16[64,128]{1,0:T(8,128)(2,1)S(1)} %reshape.182), channel_id=1, replica_groups=mesh['obs'=8,'src'=16] {'src'}, dimensions={1}, use_global_device_ids=true | all-gather | bytes 278528 | tf_op jit(solution)/shard_map/all_gather | solution.py:46
  394.8 4.7 %fusion.38 = f32[64,1024]{1,0:T(8,128)S(1)} fusion(bf16[64,2048]{1,0:T(8,128)(2,1)S(1)} %all_gather.19, pred[2048,1024]{1,0:T(32,128)(4,1)} %broadcast_in_dim.38, bf16[256,8,8,128]{3,2,1,0:T(8,128)(2,1)} %bitcast.210), kind=kOutput, calls=%fused_computation.84 | convolution fusion | flops 270532608 | bytes 6815744 | tf_op jit(solution)/shard_map/dot_general | solution.py:37
  399.6 0.9 convolution_add_fusion.1
  400.4 1.5 copy-done.9
  401.9 4.7 %fusion.11 = bf16[64,1024]{1,0:T(8,128)(2,1)S(1)} fusion(f32[64,1024]{1,0:T(8,128)S(1)} %convolution_add_fusion.1, bf16[64,2048]{1,0:T(8,128)(2,1)S(1)} %all_gather.17, pred[2048,1024]{1,0:T(32,128)(4,1)S(1)} %copy-done.12, pred[2048,1024]{1,0:T(32,128)(4,1)} %broadcast_in_dim.40, bf16[256,8,8,128]{3,2,1,0:T(8,128)(2,1)S(1)} %bitcast.205, ...), kind=kOutput, calls=%fused_computation.39 | convolution fusion | flops 272760832 | bytes 13238272 | tf_op jit(solution)/shard_map/dot_general | solution.py:37
  406.6 0.8 copy.38
  407.4 27.7 %reduce-scatter.24.cloned.1.call-done = bf16[128,64]{1,0:T(8,128)(2,1)} async-done(((bf16[1024,64]{1,0:T(8,128)(2,1)}), bf16[128,64]{1,0:T(8,128)(2,1)}) %reduce-scatter.24.cloned.1.call-update) | async-done | bytes 16400
  435.1 6.6 %fusion.6 = bf16[5,2,64,1536]{3,2,1,0:T(8,128)(2,1)} fusion(bf16[5,2,64,1536]{3,2,1,0:T(8,128)(2,1)} %get-tuple-element.19, bf16[2,1536,1536]{2,1,0:T(8,128)(2,1)} %param.11, bf16[64,2,64]{0,2,1:T(8,128)(2,1)} %bitcast.222, bf16[2,64,1536]{2,1,0:T(8,128)(2,1)S(1)} %copy-done, bf16[5,2,64,1536]{3,2,1,0:T(8,128)(2,1)} %param.8), kind=kOutput, calls=%fused_computation.24 | convolution fusion | flops 629932032 | bytes 10649600 | tf_op jit(solution)/shard_map/ceb,cbd->ced/dot_general | solution.py:57
  (54 shorter events, 1.1 us)
Async XLA Ops:
  6.5 149.3 %copy-start = (bf16[2,64,1536]{2,1,0:T(8,128)(2,1)S(1)}, bf16[2,64,1536]{2,1,0:T(8,128)(2,1)}, u32[]{:S(2)}) copy-start(bf16[2,64,1536]{2,1,0:T(8,128)(2,1)} %param.10) | copy-start | bytes 1179652
  6.5 149.3 %reduce-scatter.16.cloned.1.call-start = ((), (), s32[]{:S(2)}) async-start(), calls=%async_computation.5 | async-start | bytes 294912
  116.8 6.3 %copy-start.1 = (bf16[2048,1024]{1,0:T(8,128)(2,1)S(1)}, bf16[2048,1024]{1,0:T(8,128)(2,1)}, u32[]{:S(2)}) copy-start(bf16[2048,1024]{1,0:T(8,128)(2,1)} %select_n.103) | copy-start | bytes 12582916
  124.9 99.3 %reduce-scatter.18.cloned.1.call-start = ((), (), s32[]{:S(2)}) async-start(), calls=%async_computation.6 | async-start | bytes 294912
  155.9 6.6 %copy-start.13 = (bf16[2,64,1536]{2,1,0:T(8,128)(2,1)S(1)}, bf16[2,64,1536]{2,1,0:T(8,128)(2,1)}, u32[]{:S(2)}) copy-start(bf16[2,64,1536]{2,1,0:T(8,128)(2,1)} %param.9) | copy-start | bytes 1179652
  186.8 73.0 %copy-start.14 = (bf16[64,2048]{1,0:T(8,128)(2,1)}, bf16[64,2048]{1,0:T(8,128)(2,1)S(1)}, u32[]{:S(2)}) copy-start(bf16[64,2048]{1,0:T(8,128)(2,1)S(1)} %all_gather.16) | copy-start | bytes 786436
  186.8 4.7 %copy-start.7 = (bf16[2048,1024]{1,0:T(8,128)(2,1)S(1)}, bf16[2048,1024]{1,0:T(8,128)(2,1)}, u32[]{:S(2)}) copy-start(bf16[2048,1024]{1,0:T(8,128)(2,1)} %select_n.100) | copy-start | bytes 12582916
  191.6 2.2 copy-start.2
  195.5 96.0 %reduce-scatter.20.cloned.1.call-start = ((), (), s32[]{:S(2)}) async-start(), calls=%async_computation.7 | async-start | bytes 294912
  255.1 4.7 %copy-start.4 = (bf16[2048,1024]{1,0:T(8,128)(2,1)S(1)}, bf16[2048,1024]{1,0:T(8,128)(2,1)}, u32[]{:S(2)}) copy-start(bf16[2048,1024]{1,0:T(8,128)(2,1)} %bitcast_select_fusion.1) | copy-start | bytes 12582916
  259.8 2.2 copy-start.3
  263.8 99.9 %reduce-scatter.22.cloned.1.call-start = ((), (), s32[]{:S(2)}) async-start(), calls=%async_computation.8 | async-start | bytes 294912
  298.0 31.0 %copy-start.12 = (pred[2048,1024]{1,0:T(32,128)(4,1)S(1)}, pred[2048,1024]{1,0:T(32,128)(4,1)}, u32[]{:S(2)}) copy-start(pred[2048,1024]{1,0:T(32,128)(4,1)} %broadcast_in_dim.39) | copy-start | bytes 6291460
  322.7 0.7 copy-start.16
  323.4 4.7 %copy-start.5 = (bf16[2048,1024]{1,0:T(8,128)(2,1)S(1)}, bf16[2048,1024]{1,0:T(8,128)(2,1)}, u32[]{:S(2)}) copy-start(bf16[2048,1024]{1,0:T(8,128)(2,1)} %bitcast_select_fusion.1) | copy-start | bytes 12582916
  323.4 5.6 %copy-start.10 = (bf16[1,2048,8,1,128]{4,2,3,1,0:T(8,128)(2,1)S(1)}, bf16[1,2048,8,1,128]{4,2,3,1,0:T(8,128)(2,1)}, u32[]{:S(2)}) copy-start(bf16[1,2048,8,1,128]{4,2,3,1,0:T(8,128)(2,1)} %get-tuple-element.9) | copy-start | bytes 12582916
  328.1 2.3 copy-start.8
  328.1 2.3 copy-start.15
  336.0 99.1 %reduce-scatter.24.cloned.1.call-start = ((), (), s32[]{:S(2)}) async-start(), calls=%async_computation.9 | async-start | bytes 294912
  394.8 4.7 %copy-start.6 = (bf16[2048,1024]{1,0:T(8,128)(2,1)S(1)}, bf16[2048,1024]{1,0:T(8,128)(2,1)}, u32[]{:S(2)}) copy-start(bf16[2048,1024]{1,0:T(8,128)(2,1)} %bitcast_select_fusion.1) | copy-start | bytes 12582916
  394.8 4.7 %copy-start.17 = (bf16[64,2048]{1,0:T(8,128)(2,1)S(1)}, bf16[64,2048]{1,0:T(8,128)(2,1)}, u32[]{:S(2)}) copy-start(bf16[64,2048]{1,0:T(8,128)(2,1)} %copy-done.16) | copy-start | bytes 786436
  394.8 5.6 %copy-start.11 = (bf16[1,2048,8,1,128]{4,2,3,1,0:T(8,128)(2,1)S(1)}, bf16[1,2048,8,1,128]{4,2,3,1,0:T(8,128)(2,1)}, u32[]{:S(2)}) copy-start(bf16[1,2048,8,1,128]{4,2,3,1,0:T(8,128)(2,1)} %get-tuple-element.9) | copy-start | bytes 12582916
  399.5 2.3 copy-start.9
Sparse Core Ops, SparseCore 0:
  125.0 30.8 reduce-scatter.15
  195.6 28.4 reduce-scatter.17
  263.9 27.5 reduce-scatter.19
  336.1 27.5 reduce-scatter.21
  407.5 27.5 reduce-scatter.23
where the time goes:
time: 457 us; the launch traced here: 448 us
  blocking collectives  123 us (27%)
  local copies, waits for them, and re-layouts  120 us (26%)
  waiting for transfers between devices  89.7 us (20%)
  matrix products  78.4 us (17%)
  other arithmetic  23.2 us (5%)
  between operations  13.7 us (3%)
    all_gather x4, blocking collectives, per_device(): newest = lax.all_gather(latest, 'src', axis=1, tiled=True)  96.4 us
    unnamed x10, waiting for transfers between devices  89.7 us
    broadcast_in_dim x6, local copies, waits for them, and re-layouts, per_device(): combined = jnp.where(chosen, kernel[tap_index], combined)  44.7 us
    dot_general x15, matrix products, couple(): jnp.dot(columns, matrices[delay - 1], preferred_element_type=jnp.float32)  40.5 us
    select_n x3, local copies, waits for them, and re-layouts, per_device(): combined = jnp.where(chosen, kernel[tap_index], combined)  35.6 us
    dot_general x5, matrix products, per_device(): jnp.einsum('ceb,cbd->ced', residual_field, near_inverse, preferred_elemen...  32.8 us
    all_gather x1, blocking collectives, per_device(): gathered = lax.all_gather(stacked, 'src', axis=2, tiled=True)  26.3 us
    select_n x2, other arithmetic, per_device(): combined = jnp.where(chosen, kernel[tap_index], combined)  22.5 us
  transfers between devices with their start and end apart: 5, of which 5 were waited for; matrix products, arithmetic and copies ran while one was open for 12% of the time, Pallas kernels for 0%

commit v1 on v0

v1 whole, which is shorter than its diff:
```python
import jax
import jax.numpy as jnp
from jax import lax
from jax.experimental import pallas as pl
from jax.experimental.pallas import tpu as pltpu
from jax.sharding import PartitionSpec as P

STEPS = 5
HIST = 3
MIB = 1024 * 1024
BF16 = jnp.bfloat16
F32 = jnp.float32
VMEM_SPEC = pl.BlockSpec(memory_space=pltpu.VMEM)


def nt_dot(left, right):
    return lax.dot_general(left, right, (((1,), (1,)), ((), ())), preferred_element_type=F32)


def params(limit, **more):
    return pltpu.CompilerParams(vmem_limit_bytes=limit * MIB, **more)


def cost(flops, touched):
    return pl.CostEstimate(flops=int(flops), bytes_accessed=int(touched), transcendentals=0)


def history_kernel(history_ref, proj_ref, out_ref):
    slots, clusters, excite, unknowns = history_ref.shape
    parts = []
    for c in range(clusters):
        left = jnp.concatenate([history_ref[h, c] for h in range(slots)], axis=0)
        parts.append(nt_dot(left, proj_ref[c]))
    both = jnp.concatenate(parts, axis=1).astype(BF16)
    for s in range(out_ref.shape[0]):
        for h in range(slots):
            out_ref[s, h] = both[h * excite:(h + 1) * excite]


def project_history(history, proj_basis, copies):
    slots, clusters, excite, unknowns = history.shape
    rank = proj_basis.shape[1]
    return pl.pallas_call(
        history_kernel,
        out_shape=jax.ShapeDtypeStruct((copies, slots, excite, clusters * rank), BF16),
        in_specs=[VMEM_SPEC] * 2,
        out_specs=VMEM_SPEC,
        compiler_params=params(16),
        name="project_history",
    )(history, proj_basis)


def near_kernel(incident_ref, expand_ref, near_ref, proj_ref,
                incoming_ref, expanded_ref, start_ref, transfer_ref, acc_ref):
    c, n = pl.program_id(0), pl.program_id(1)
    steps, _, excite, unknowns = incident_ref.shape
    rank = expand_ref.shape[1]
    left = jnp.concatenate([incident_ref[t, 0] for t in range(steps)] + [expand_ref[0]], axis=0)
    product = jnp.dot(left, near_ref[0], preferred_element_type=F32).astype(BF16)
    for t in range(steps):
        incoming_ref[t, 0] = product[t * excite:(t + 1) * excite]
    expanded_ref[0] = product[steps * excite:]
    small = nt_dot(product, proj_ref[0])

    @pl.when(n == 0)
    def _():
        acc_ref[c] = small

    @pl.when(n > 0)
    def _():
        acc_ref[c] += small

    @pl.when((c == 1) & (n == pl.num_programs(1) - 1))
    def _():
        for t in range(steps):
            rows = slice(t * excite, (t + 1) * excite)
            start_ref[t] = jnp.concatenate([acc_ref[0, rows], acc_ref[1, rows]], axis=1)
        tail = slice(steps * excite, steps * excite + rank)
        zero = jnp.zeros((rank, rank), F32)
        full = jnp.concatenate([
            jnp.concatenate([acc_ref[0, tail], zero], axis=1),
            jnp.concatenate([zero, acc_ref[1, tail]], axis=1),
        ], axis=0)
        high = full.astype(BF16)
        low = (full - high.astype(F32)).astype(BF16)
        transfer_ref[...] = jnp.concatenate([high, low], axis=0)


def prepare_near(incident, expand_basis, near_inverse, proj_basis, tile=512):
    steps, clusters, excite, unknowns = incident.shape
    rank = proj_basis.shape[1]
    rows = steps * excite + rank
    return pl.pallas_call(
        near_kernel,
        grid=(clusters, unknowns // tile),
        out_shape=(
            jax.ShapeDtypeStruct((steps, clusters, excite, unknowns), BF16),
            jax.ShapeDtypeStruct((clusters, rank, unknowns), BF16),
            jax.ShapeDtypeStruct((steps, excite, clusters * rank), F32),
            jax.ShapeDtypeStruct((2 * clusters * rank, clusters * rank), BF16),
        ),
        in_specs=[
            pl.BlockSpec((steps, 1, excite, unknowns), lambda c, n: (0, c, 0, 0)),
            pl.BlockSpec((1, rank, unknowns), lambda c, n: (c, 0, 0)),
            pl.BlockSpec((1, unknowns, tile), lambda c, n: (c, 0, n)),
            pl.BlockSpec((1, rank, tile), lambda c, n: (c, 0, n)),
        ],
        out_specs=(
            pl.BlockSpec((steps, 1, excite, tile), lambda c, n: (0, c, 0, n)),
            pl.BlockSpec((1, rank, tile), lambda c, n: (c, 0, n)),
            pl.BlockSpec((steps, excite, clusters * rank), lambda c, n: (0, 0, 0)),
            pl.BlockSpec((2 * clusters * rank, clusters * rank), lambda c, n: (0, 0)),
        ),
        scratch_shapes=[pltpu.VMEM((clusters, rows, rank), F32)],
        compiler_params=params(24),
        cost_estimate=cost(2 * clusters * rows * unknowns * (unknowns + rank), 2 * clusters * unknowns * unknowns),
        name="prepare_near",
    )(incident, expand_basis, near_inverse, proj_basis)


def first_kernel(gathered_ref, couplings_ref, lags_ref,
                 w1_ref, w2_ref, w3_ref, field_ref, base_ref, perm_ref, acc_ref):
    i = pl.program_id(0)
    blocks = lags_ref.shape[1] // 128
    rows_in = 256
    group = rows_in // blocks
    rank = 64
    clusters_here = w1_ref.shape[0] // rank
    excite = gathered_ref.shape[2]

    @pl.when(i == 0)
    def _():
        to = lax.broadcasted_iota(jnp.int32, (rows_in, rows_in), 0)
        source = lax.broadcasted_iota(jnp.int32, (rows_in, rows_in), 1)
        wanted = (to % group) * blocks + to // group
        perm_ref[...] = jnp.where(source == wanted, 1.0, 0.0).astype(BF16)
        acc_ref[...] = jnp.zeros_like(acc_ref)

    perm = perm_ref[...]

    @pl.loop(0, clusters_here)
    def _(j):
        lag = lags_ref[pl.ds(i * clusters_here + j, 1), :]
        masks = []
        for wanted in (1.0, 2.0):
            row = jnp.where(lag == wanted, 1.0, 0.0)
            masks.append([
                jnp.broadcast_to(row[:, o * 128:(o + 1) * 128], (group, 128)).astype(BF16)
                for o in range(blocks)
            ])
        for g in range(rank // group):
            at = pl.multiple_of(j * (rank * blocks) + g * rows_in, rows_in)
            pair = jnp.concatenate(
                [couplings_ref[p, pl.ds(at, rows_in), :] for p in range(2)], axis=1)
            sorted_pair = jnp.dot(perm, pair, preferred_element_type=F32).astype(BF16)
            out = pl.ds(pl.multiple_of(j * rank + g * group, group), group)
            for o in range(blocks):
                k0 = sorted_pair[o * group:(o + 1) * group, :128]
                k1 = sorted_pair[o * group:(o + 1) * group, 128:]
                m1, m2 = masks[0][o], masks[1][o]
                lanes = slice(o * 128, (o + 1) * 128)
                w1_ref[out, lanes] = k0 * m1
                w2_ref[out, lanes] = k0 * m2 + k1 * m1
                w3_ref[out, lanes] = k1 * m2

    def left(h):
        return jnp.concatenate([gathered_ref[0, h], gathered_ref[1, h]], axis=1)

    old, middle, new = left(0), left(1), left(2)
    one = jnp.dot(new, w1_ref[...], preferred_element_type=F32)
    two = jnp.dot(jnp.concatenate([middle, new], axis=0), w2_ref[...], preferred_element_type=F32)
    three = jnp.dot(jnp.concatenate([old, middle, new], axis=0), w3_ref[...], preferred_element_type=F32)
    acc_ref[0] += one + two[:excite] + three[:excite]
    acc_ref[1] += two[excite:] + three[excite:2 * excite]
    acc_ref[2] += three[2 * excite:]

    @pl.when(i == pl.num_programs(0) - 1)
    def _():
        for o in range(blocks):
            field_ref[o] = acc_ref[0, :, o * 128:(o + 1) * 128].astype(BF16)
        base_ref[0] = acc_ref[1]
        base_ref[1] = acc_ref[2]


def first_step(gathered, couplings, lag_rows):
    senders, slots, excite, width = gathered.shape
    clusters, columns = lag_rows.shape
    rows = senders * width
    blocks = columns // 128
    steps = 8
    part = rows // steps
    matrix = jax.ShapeDtypeStruct((rows, columns), BF16)
    return pl.pallas_call(
        first_kernel,
        grid=(steps,),
        out_shape=(
            matrix, matrix, matrix,
            jax.ShapeDtypeStruct((blocks, excite, 128), BF16),
            jax.ShapeDtypeStruct((2, excite, columns), F32),
        ),
        in_specs=[
            pl.BlockSpec((senders // steps, slots, excite, width), lambda i: (i, 0, 0, 0)),
            pl.BlockSpec((2, part * blocks, 128), lambda i: (0, i, 0)),
            pl.BlockSpec((clusters, columns), lambda i: (0, 0)),
        ],
        out_specs=(
            pl.BlockSpec((part, columns), lambda i: (i, 0)),
            pl.BlockSpec((part, columns), lambda i: (i, 0)),
            pl.BlockSpec((part, columns), lambda i: (i, 0)),
            pl.BlockSpec((blocks, excite, 128), lambda i: (0, 0, 0)),
            pl.BlockSpec((2, excite, columns), lambda i: (0, 0, 0)),
        ),
        scratch_shapes=[
            pltpu.VMEM((256, 256), BF16),
            pltpu.VMEM((3, excite, columns), F32),
        ],
        compiler_params=params(24),
        cost_estimate=cost(2 * 6 * excite * rows * columns, 10 * rows * columns),
        name="first_step",
    )(gathered, couplings, lag_rows)


def wide(gathered_ref):
    return jnp.concatenate([gathered_ref[s] for s in range(gathered_ref.shape[0])], axis=1)


def send_field(field_ref, total):
    for o in range(field_ref.shape[0]):
        field_ref[o] = total[:, o * 128:(o + 1) * 128].astype(BF16)


def step1_kernel(q0_ref, base_ref, w1_ref, field_ref):
    send_field(field_ref, base_ref[0] + jnp.dot(wide(q0_ref), w1_ref[...], preferred_element_type=F32))


def step2_kernel(q0_ref, q1_ref, base_ref, w1_ref, w2_ref, field_ref, next_ref):
    excite = base_ref.shape[1]
    one, zero = wide(q1_ref), wide(q0_ref)
    two = jnp.dot(jnp.concatenate([zero, one], axis=0), w2_ref[...], preferred_element_type=F32)
    send_field(field_ref, base_ref[1] + two[:excite] + jnp.dot(one, w1_ref[...], preferred_element_type=F32))
    next_ref[...] = two[excite:]


def step3_kernel(q0_ref, q1_ref, q2_ref, base_ref, w1_ref, w3_ref, field_ref, next_ref):
    excite = base_ref.shape[0]
    three = jnp.dot(jnp.concatenate([wide(q0_ref), wide(q1_ref)], axis=0), w3_ref[...], preferred_element_type=F32)
    send_field(field_ref, base_ref[...] + three[:excite]
               + jnp.dot(wide(q2_ref), w1_ref[...], preferred_element_type=F32))
    next_ref[...] = three[excite:]


def step4_kernel(q2_ref, q3_ref, base_ref, w1_ref, w2_ref, field_ref):
    send_field(field_ref, base_ref[...]
               + jnp.dot(wide(q2_ref), w2_ref[...], preferred_element_type=F32)
               + jnp.dot(wide(q3_ref), w1_ref[...], preferred_element_type=F32))


def couple(kernel, name, blocks, with_next, *arrays):
    excite, width = arrays[0].shape[1:]
    shapes = [jax.ShapeDtypeStruct((blocks, excite, width), BF16)]
    if with_next:
        shapes.append(jax.ShapeDtypeStruct((excite, blocks * width), F32))
    got = pl.pallas_call(
        kernel,
        out_shape=shapes,
        in_specs=[VMEM_SPEC] * len(arrays),
        out_specs=[VMEM_SPEC] * len(shapes),
        compiler_params=params(24),
        name=name,
    )(*arrays)
    return got if with_next else got[0]


def project_kernel(parts_ref, start_ref, transfer_ref, field_ref, out_ref):
    total = parts_ref[0].astype(F32)
    for o in range(1, parts_ref.shape[0]):
        total = total + parts_ref[o].astype(F32)
    field = total.astype(BF16)
    field_ref[...] = field
    q = start_ref[0] - jnp.dot(
        jnp.concatenate([field, field], axis=1), transfer_ref[...], preferred_element_type=F32)
    q = q.astype(BF16)
    for s in range(out_ref.shape[0]):
        out_ref[s] = q


def project_step(parts, start, transfer, copies, step):
    blocks, excite, width = parts.shape
    return pl.pallas_call(
        project_kernel,
        grid=(1,),
        out_shape=(
            jax.ShapeDtypeStruct((excite, width), BF16),
            jax.ShapeDtypeStruct((copies, excite, width), BF16),
        ),
        in_specs=[
            pl.BlockSpec(parts.shape, lambda i: (0, 0, 0)),
            pl.BlockSpec((1, excite, width), lambda i: (step, 0, 0)),
            pl.BlockSpec(transfer.shape, lambda i: (0, 0)),
        ],
        out_specs=(
            pl.BlockSpec((excite, width), lambda i: (0, 0)),
            pl.BlockSpec((copies, excite, width), lambda i: (0, 0, 0)),
        ),
        compiler_params=params(8),
        name="project_step",
    )(parts, start, transfer)


def currents_kernel(incoming_ref, expanded_ref, parts_ref, f0_ref, f1_ref, f2_ref, f3_ref, out_ref):
    total = parts_ref[0].astype(F32)
    for o in range(1, parts_ref.shape[0]):
        total = total + parts_ref[o].astype(F32)
    fields = [f0_ref[...], f1_ref[...], f2_ref[...], f3_ref[...], total.astype(BF16)]
    excite = out_ref.shape[2]
    rank = expanded_ref.shape[1]
    for c in range(out_ref.shape[1]):
        left = jnp.concatenate([f[:, c * rank:(c + 1) * rank] for f in fields], axis=0)
        far = jnp.dot(left, expanded_ref[c], preferred_element_type=F32)
        for t in range(out_ref.shape[0]):
            out_ref[t, c] = (incoming_ref[t, c].astype(F32) - far[t * excite:(t + 1) * excite]).astype(BF16)


def final_currents(incoming, expanded, parts, fields, tile=512):
    steps, clusters, excite, unknowns = incoming.shape
    rank = expanded.shape[1]
    small = pl.BlockSpec(fields[0].shape, lambda n: (0, 0))
    return pl.pallas_call(
        currents_kernel,
        grid=(unknowns // tile,),
        out_shape=jax.ShapeDtypeStruct(incoming.shape, BF16),
        in_specs=[
            pl.BlockSpec((steps, clusters, excite, tile), lambda n: (0, 0, 0, n)),
            pl.BlockSpec((clusters, rank, tile), lambda n: (0, 0, n)),
            pl.BlockSpec(parts.shape, lambda n: (0, 0, 0)),
        ] + [small] * len(fields),
        out_specs=pl.BlockSpec((steps, clusters, excite, tile), lambda n: (0, 0, 0, n)),
        compiler_params=params(16),
        name="final_currents",
    )(incoming, expanded, parts, *fields)


def per_device(history, incident, proj_basis, expand_basis, near_inverse, couplings, lags):
    clusters, rank, unknowns = proj_basis.shape
    width = clusters * rank
    taps, src_rows, blocks = couplings.shape[:3]
    src_clusters = lags.shape[0]
    senders = src_rows // width
    flat = couplings.reshape(taps, src_rows * blocks, width)
    spread = jnp.repeat(jnp.eye(blocks * clusters, dtype=F32), rank, axis=1)
    lag_rows = jnp.dot(lags.reshape(src_clusters, blocks * clusters).astype(F32), spread)

    def gather(copies):
        return lax.all_to_all(copies, "src", 0, 0)

    def scatter(chunks):
        return lax.all_to_all(chunks, "obs", 0, 0)

    gathered = gather(project_history(history, proj_basis, senders))
    incoming, expanded, start, transfer = prepare_near(incident, expand_basis, near_inverse, proj_basis)
    w1, w2, w3, chunks, base = first_step(gathered, flat, lag_rows)
    fields, past = [], []
    ahead = None
    for step in range(STEPS):
        if step == 1:
            chunks = couple(step1_kernel, "step1", blocks, False, past[0], base, w1)
        elif step == 2:
            chunks, ahead = couple(step2_kernel, "step2", blocks, True, past[0], past[1], base, w1, w2)
        elif step == 3:
            chunks, ahead = couple(step3_kernel, "step3", blocks, True, *past, ahead, w1, w3)
        elif step == 4:
            chunks = couple(step4_kernel, "step4", blocks, False, past[2], past[3], ahead, w1, w2)
        parts = scatter(chunks)
        if step + 1 < STEPS:
            field, copies = project_step(parts, start, transfer, senders, step)
            fields.append(field)
            past.append(gather(copies))
    return final_currents(incoming, expanded, parts, fields)


def solution(mesh):
    placed = (
        P(None, ("obs", "src"), None, None),
        P(None, ("obs", "src"), None, None),
        P(("obs", "src"), None, None),
        P(("obs", "src"), None, None),
        P(("obs", "src"), None, None),
        P(None, "obs", None, "src", None),
        P("obs", None, "src", None),
    )
    return jax.shard_map(
        per_device,
        mesh=mesh,
        in_specs=placed,
        out_specs=P(None, ("obs", "src"), None, None),
        check_vma=False,
    )
```

time: 457 us -> 163 us (0.36); the launches traced: 448 us -> 162 us
  local copies, waits for them, and re-layouts: 120 us -> 21.9 us
  matrix products: 78.4 us -> 0.21 us
  waiting for transfers between devices: 89.7 us -> 13.4 us
  blocking collectives: 123 us -> 83.1 us
  Pallas kernels: 0 us -> 30.1 us
  other arithmetic: 23.2 us -> 0.71 us
  between operations: 13.7 us -> 0.12 us
  starting transfers between devices: 0.99 us -> 12.4 us
    all_gather x5 -> x0, blocking collectives: 123 us -> none  [the longest x4 96.4 us: per_device(): newest = lax.all_gather(latest, 'src', axis=1, tiled=True)]
    unnamed x10 -> x0, waiting for transfers between devices: 89.7 us -> none
    all_to_all x0 -> x8, blocking collectives: none -> 83.1 us  [the longest x4 47 us: gather(): return lax.all_to_all(copies, 'src', 0, 0)]
    dot_general x27 -> x1, matrix products: 78.4 us -> 0.21 us  [per_device(): jnp.dot(lags.reshape(src_clusters, blocks * clusters).astype(F32), spread)]
    broadcast_in_dim x6 -> x1, local copies, waits for them, and re-layouts: 44.7 us -> 0.1 us  [per_device(): spread = jnp.repeat(jnp.eye(blocks * clusters, dtype=F32), rank, axis=1)]
    select_n x3 -> x0, local copies, waits for them, and re-layouts: 35.6 us -> none  [per_device(): combined = jnp.where(chosen, kernel[tap_index], combined)]
    pallas_call x0 -> x12, Pallas kernels: none -> 30.1 us  [the longest x1 13.1 us: first_step(): pl.pallas_call(first_kernel, grid=(steps,), out_shape=(matrix, matrix, ma...]
    select_n x2 -> x0, other arithmetic: 22.5 us -> none  [per_device(): combined = jnp.where(chosen, kernel[tap_index], combined)]
  transfers between devices with their start and end apart: 5 -> 2, of which waited for: 5 -> 1; matrix products, arithmetic and copies ran while one was open for 12% -> 1% of each run, Pallas kernels for 0% -> 5%
where the time goes in v1:
time: 163 us; the launch traced here: 162 us
  blocking collectives  83.1 us (51%)
  Pallas kernels  30.1 us (18%)
  local copies, waits for them, and re-layouts  21.9 us (13%)
  waiting for transfers between devices  13.4 us (8%)
  starting transfers between devices  12.4 us (8%)
    all_to_all x4, blocking collectives, gather(): return lax.all_to_all(copies, 'src', 0, 0)  47 us
    all_to_all x4, blocking collectives, scatter(): return lax.all_to_all(chunks, 'obs', 0, 0)  36.1 us
    unnamed x30, local copies, waits for them, and re-layouts  21.7 us
    all_to_all x1, waiting for transfers between devices, gather(): return lax.all_to_all(copies, 'src', 0, 0)  13.4 us
    pallas_call x1, Pallas kernels, first_step(): pl.pallas_call(first_kernel, grid=(steps,), out_shape=(matrix, matrix, ma...  13.1 us
    pallas_call x1, Pallas kernels, prepare_near(): pl.pallas_call(near_kernel, grid=(clusters, unknowns // tile), out_shape=...  7.35 us
    all_to_all x1, starting transfers between devices, gather(): return lax.all_to_all(copies, 'src', 0, 0)  7.12 us
    all_to_all x1, starting transfers between devices, scatter(): return lax.all_to_all(chunks, 'obs', 0, 0)  5.31 us
  transfers between devices with their start and end apart: 2, of which 1 were waited for; matrix products, arithmetic and copies ran while one was open for 1% of the time, Pallas kernels for 5%

profile of v1, /device:TPU:0, one launch (start us, length us, event | category | flops | bytes accessed | tf_op | source)
XLA Modules:
  0.0 162.0 jit_solution(11229159162887161278)
XLA Ops:
  0.0 0.0 copy-start.7
  0.0 1.3 copy-done.7
  1.3 0.0 copy-start.8
  1.3 1.0 copy-done.8
  2.3 1.4 project_history.1
  3.7 7.1 %all-to-all-start = ((bf16[16,3,64,128]{3,2,1,0:T(8,128)(2,1)}), bf16[16,3,64,128]{3,2,1,0:T(8,128)(2,1)S(1)}, u32[]{:S(2)}, u32[]{:S(2)}) async-start(bf16[16,3,64,128]{3,2,1,0:T(8,128)(2,1)} %project_history.1), calls=%async_computation | async-start | bytes 1572864 | tf_op jit(solution)/shard_map/all_to_all | solution.py:354
  10.8 0.7 convert_element_type.10
  11.5 0.1 broadcast_in_dim.3
  11.6 0.1 reshape.9
  11.8 0.2 convolution_bitcast_fusion.lags_ref
  12.0 13.4 %all-to-all-done.gathered_ref = bf16[16,3,64,128]{3,2,1,0:T(8,128)(2,1)S(1)} async-done(((bf16[16,3,64,128]{3,2,1,0:T(8,128)(2,1)}), bf16[16,3,64,128]{3,2,1,0:T(8,128)(2,1)S(1)}, u32[]{:S(2)}, u32[]{:S(2)}) %all-to-all-start) | async-done | bytes 786464 | tf_op jit(solution)/shard_map/all_to_all | solution.py:354
  25.3 0.0 copy-start.4
  25.3 3.4 %copy-done.4 = bf16[2,2048,8,1,128]{4,2,3,1,0:T(8,128)(2,1)S(1)} copy-done((bf16[2,2048,8,1,128]{4,2,3,1,0:T(8,128)(2,1)S(1)}, bf16[2,2048,8,1,128]{4,2,3,1,0:T(8,128)(2,1)}, u32[]{:S(2)}) %copy-start.4) | copy-done | bytes 8388632
  28.7 13.1 %first_step.1 = (bf16[2048,1024]{1,0:T(8,128)(2,1)S(1)}, bf16[2048,1024]{1,0:T(8,128)(2,1)S(1)}, bf16[2048,1024]{1,0:T(8,128)(2,1)S(1)}, bf16[8,64,128]{2,1,0:T(8,128)(2,1)}, f32[2,64,1024]{2,1,0:T(8,128)S(1)}) custom-call(bf16[16,3,64,128]{3,2,1,0:T(8,128)(2,1)S(1)} %all-to-all-done.gathered_ref, bf16[2,16384,128]{2,1,0:T(8,128)(2,1)S(1)} %bitcast.6, ...), custom_call_target="tpu_custom_call" | custom-call | flops 1610612736 | bytes 20971520 | tf_op jit(solution)/shard_map/first_step/pallas_call | solution.py:193
  41.8 0.0 copy-start
  41.8 1.9 %copy-done = bf16[2048,1024]{1,0:T(8,128)(2,1)} copy-done((bf16[2048,1024]{1,0:T(8,128)(2,1)}, bf16[2048,1024]{1,0:T(8,128)(2,1)S(1)}, u32[]{:S(2)}) %copy-start) | copy-done | bytes 4194328
  43.7 0.0 copy-start.2
  43.7 2.0 %copy-done.2 = bf16[2048,1024]{1,0:T(8,128)(2,1)} copy-done((bf16[2048,1024]{1,0:T(8,128)(2,1)}, bf16[2048,1024]{1,0:T(8,128)(2,1)S(1)}, u32[]{:S(2)}) %copy-start.2) | copy-done | bytes 4194328
  45.8 0.0 copy-start.5
  45.8 2.0 %copy-done.5 = bf16[2048,1024]{1,0:T(8,128)(2,1)} copy-done((bf16[2048,1024]{1,0:T(8,128)(2,1)}, bf16[2048,1024]{1,0:T(8,128)(2,1)S(1)}, u32[]{:S(2)}) %copy-start.5) | copy-done | bytes 4194328
  47.7 5.3 %all-to-all-start.1 = ((bf16[8,64,128]{2,1,0:T(8,128)(2,1)}), bf16[8,64,128]{2,1,0:T(8,128)(2,1)S(1)}, u32[]{:S(2)}, u32[]{:S(2)}) async-start(bf16[8,64,128]{2,1,0:T(8,128)(2,1)} %get-tuple-element.28), calls=%async_computation.1 | async-start | bytes 262144 | tf_op jit(solution)/shard_map/all_to_all | solution.py:357
  53.1 0.0 copy-start.9
  53.1 1.0 copy-done.9
  54.1 0.0 copy-start.12
  54.1 3.7 %copy-done.12 = bf16[2,1536,1536]{2,1,0:T(8,128)(2,1)S(1)} copy-done((bf16[2,1536,1536]{2,1,0:T(8,128)(2,1)S(1)}, bf16[2,1536,1536]{2,1,0:T(8,128)(2,1)}, u32[]{:S(2)}) %copy-start.12) | copy-done | bytes 9437208
  57.7 0.0 copy-start.13
  57.7 1.5 copy-done.13
  59.3 0.0 copy-start.14
  59.3 1.0 copy-done.14
  60.3 7.4 %prepare_near.1 = (bf16[5,2,64,1536]{3,2,1,0:T(8,128)(2,1)S(1)}, bf16[2,64,1536]{2,1,0:T(8,128)(2,1)S(1)}, f32[5,64,128]{2,1,0:T(8,128)S(1)}, bf16[256,128]{1,0:T(8,128)(2,1)S(1)}) custom-call(bf16[5,2,64,1536]{3,2,1,0:T(8,128)(2,1)S(1)} %copy-done.13, bf16[2,64,1536]{2,1,0:T(8,128)(2,1)S(1)} %copy-done.14, bf16[2,1536,1536]{2,1,0:T(8,128)(2,1)S(1)} %copy-done.12, ...), custom_call_target="tpu_custom_call" | custom-call | flops 3774873600 | bytes 9437184 | tf_op jit(solution)/shard_map/prepare_near/pallas_call | solution.py:93
  67.6 0.0 copy-start.10
  67.7 0.7 copy-done.10
  68.4 0.0 all-to-all-done.1.parts_ref
  68.4 0.2 project_step.4
  68.6 12.2 %all_to_all.50.q0_ref = bf16[16,64,128]{2,1,0:T(8,128)(2,1)S(1)} all-to-all(bf16[16,64,128]{2,1,0:T(8,128)(2,1)S(1)} %get-tuple-element.31), channel_id=1, replica_groups=mesh['obs'=8,'src'=16] {'src'}, dimensions={0} | all-to-all | bytes 524288 | tf_op jit(solution)/shard_map/all_to_all | solution.py:354
  80.8 0.0 copy-start.1
  80.8 2.2 %copy-done.1 = bf16[2048,1024]{1,0:T(8,128)(2,1)S(1)} copy-done((bf16[2048,1024]{1,0:T(8,128)(2,1)S(1)}, bf16[2048,1024]{1,0:T(8,128)(2,1)}, u32[]{:S(2)}) %copy-start.1) | copy-done | bytes 4194328
  83.0 0.0 copy-start.3
  83.0 0.8 step1.1
  83.8 10.5 %all_to_all.51.parts_ref = bf16[8,64,128]{2,1,0:T(8,128)(2,1)S(1)} all-to-all(bf16[8,64,128]{2,1,0:T(8,128)(2,1)S(1)} %step1.1), channel_id=1, replica_groups=mesh['obs'=8,'src'=16] {'obs'}, dimensions={0} | all-to-all | bytes 262144 | tf_op jit(solution)/shard_map/all_to_all | solution.py:357
  94.3 0.2 project_step.5
  94.5 11.6 %all_to_all.52.q1_ref = bf16[16,64,128]{2,1,0:T(8,128)(2,1)S(1)} all-to-all(bf16[16,64,128]{2,1,0:T(8,128)(2,1)S(1)} %get-tuple-element.34), channel_id=1, replica_groups=mesh['obs'=8,'src'=16] {'src'}, dimensions={0} | all-to-all | bytes 524288 | tf_op jit(solution)/shard_map/all_to_all | solution.py:354
  106.1 0.0 copy-done.3
  106.1 0.0 copy-start.6
  106.1 1.4 step2.1
  107.5 8.5 %all_to_all.53.parts_ref = bf16[8,64,128]{2,1,0:T(8,128)(2,1)S(1)} all-to-all(bf16[8,64,128]{2,1,0:T(8,128)(2,1)S(1)} %get-tuple-element.36), channel_id=1, replica_groups=mesh['obs'=8,'src'=16] {'obs'}, dimensions={0} | all-to-all | bytes 262144 | tf_op jit(solution)/shard_map/all_to_all | solution.py:357
  116.0 0.2 project_step.6
  116.2 11.6 %all_to_all.54.q2_ref = bf16[16,64,128]{2,1,0:T(8,128)(2,1)S(1)} all-to-all(bf16[16,64,128]{2,1,0:T(8,128)(2,1)S(1)} %get-tuple-element.37), channel_id=1, replica_groups=mesh['obs'=8,'src'=16] {'src'}, dimensions={0} | all-to-all | bytes 524288 | tf_op jit(solution)/shard_map/all_to_all | solution.py:354
  127.8 0.0 copy-done.6
  127.8 1.4 step3.1
  129.2 8.5 %all_to_all.55.parts_ref = bf16[8,64,128]{2,1,0:T(8,128)(2,1)S(1)} all-to-all(bf16[8,64,128]{2,1,0:T(8,128)(2,1)S(1)} %get-tuple-element.40), channel_id=1, replica_groups=mesh['obs'=8,'src'=16] {'obs'}, dimensions={0} | all-to-all | bytes 262144 | tf_op jit(solution)/shard_map/all_to_all | solution.py:357
  137.7 0.2 project_step.7
  137.9 11.6 %all_to_all.56.q3_ref = bf16[16,64,128]{2,1,0:T(8,128)(2,1)S(1)} all-to-all(bf16[16,64,128]{2,1,0:T(8,128)(2,1)S(1)} %get-tuple-element.41), channel_id=1, replica_groups=mesh['obs'=8,'src'=16] {'src'}, dimensions={0} | all-to-all | bytes 524288 | tf_op jit(solution)/shard_map/all_to_all | solution.py:354
  149.5 0.0 copy-start.11
  149.5 1.6 step4.1
  151.0 8.5 %all_to_all.57.parts_ref = bf16[8,64,128]{2,1,0:T(8,128)(2,1)S(1)} all-to-all(bf16[8,64,128]{2,1,0:T(8,128)(2,1)S(1)} %step4.1), channel_id=1, replica_groups=mesh['obs'=8,'src'=16] {'obs'}, dimensions={0} | all-to-all | bytes 262144 | tf_op jit(solution)/shard_map/all_to_all | solution.py:357
  159.5 0.0 copy-done.11
  159.6 2.4 %final_currents.1 = bf16[5,2,64,1536]{3,2,1,0:T(8,128)(2,1)} custom-call(bf16[5,2,64,1536]{3,2,1,0:T(8,128)(2,1)S(1)} %get-tuple-element.26.incoming_ref, bf16[2,64,1536]{2,1,0:T(8,128)(2,1)S(1)} %copy-done.11, bf16[8,64,128]{2,1,0:T(8,128)(2,1)S(1)} %all_to_all.57.parts_ref, bf16[64,128]{1,0:T(8,128)(2,1)S(1)} %get-tuple-element.43.f0_ref, ...), custom_call_target="tpu_custom_call" | custom-call | tf_op jit(solution)/shard_map/final_currents/pallas_call | solution.py:328
  (1 shorter events, 0.0 us)
Async XLA Ops:
  0.0 1.3 copy-start.7
  1.3 1.0 copy-start.8
  3.7 21.6 %all-to-all-start = ((bf16[16,3,64,128]{3,2,1,0:T(8,128)(2,1)}), bf16[16,3,64,128]{3,2,1,0:T(8,128)(2,1)S(1)}, u32[]{:S(2)}, u32[]{:S(2)}) async-start(bf16[16,3,64,128]{3,2,1,0:T(8,128)(2,1)} %project_history.1), calls=%async_computation | async-start | bytes 1572864 | tf_op jit(solution)/shard_map/all_to_all | solution.py:354
  25.3 3.4 %copy-start.4 = (bf16[2,2048,8,1,128]{4,2,3,1,0:T(8,128)(2,1)S(1)}, bf16[2,2048,8,1,128]{4,2,3,1,0:T(8,128)(2,1)}, u32[]{:S(2)}) copy-start(bf16[2,2048,8,1,128]{4,2,3,1,0:T(8,128)(2,1)} %param.12) | copy-start | bytes 25165828
  41.8 1.9 %copy-start = (bf16[2048,1024]{1,0:T(8,128)(2,1)}, bf16[2048,1024]{1,0:T(8,128)(2,1)S(1)}, u32[]{:S(2)}) copy-start(bf16[2048,1024]{1,0:T(8,128)(2,1)S(1)} %get-tuple-element.33.w1_ref) | copy-start | bytes 12582916
  43.7 2.0 %copy-start.2 = (bf16[2048,1024]{1,0:T(8,128)(2,1)}, bf16[2048,1024]{1,0:T(8,128)(2,1)S(1)}, u32[]{:S(2)}) copy-start(bf16[2048,1024]{1,0:T(8,128)(2,1)S(1)} %get-tuple-element.35.w2_ref) | copy-start | bytes 12582916
  45.8 2.0 %copy-start.5 = (bf16[2048,1024]{1,0:T(8,128)(2,1)}, bf16[2048,1024]{1,0:T(8,128)(2,1)S(1)}, u32[]{:S(2)}) copy-start(bf16[2048,1024]{1,0:T(8,128)(2,1)S(1)} %get-tuple-element.39.w3_ref) | copy-start | bytes 12582916
  47.7 20.6 %all-to-all-start.1 = ((bf16[8,64,128]{2,1,0:T(8,128)(2,1)}), bf16[8,64,128]{2,1,0:T(8,128)(2,1)S(1)}, u32[]{:S(2)}, u32[]{:S(2)}) async-start(bf16[8,64,128]{2,1,0:T(8,128)(2,1)} %get-tuple-element.28), calls=%async_computation.1 | async-start | bytes 262144 | tf_op jit(solution)/shard_map/all_to_all | solution.py:357
  53.1 1.0 copy-start.9
  54.1 3.7 %copy-start.12 = (bf16[2,1536,1536]{2,1,0:T(8,128)(2,1)S(1)}, bf16[2,1536,1536]{2,1,0:T(8,128)(2,1)}, u32[]{:S(2)}) copy-start(bf16[2,1536,1536]{2,1,0:T(8,128)(2,1)} %near_ref.1) | copy-start | bytes 28311556
  57.7 1.5 copy-start.13
  59.3 1.0 copy-start.14
  67.6 0.7 copy-start.10
  80.8 2.2 %copy-start.1 = (bf16[2048,1024]{1,0:T(8,128)(2,1)S(1)}, bf16[2048,1024]{1,0:T(8,128)(2,1)}, u32[]{:S(2)}) copy-start(bf16[2048,1024]{1,0:T(8,128)(2,1)} %copy-done) | copy-start | bytes 12582916
  83.0 23.1 %copy-start.3 = (bf16[2048,1024]{1,0:T(8,128)(2,1)S(1)}, bf16[2048,1024]{1,0:T(8,128)(2,1)}, u32[]{:S(2)}) copy-start(bf16[2048,1024]{1,0:T(8,128)(2,1)} %copy-done.2) | copy-start | bytes 12582916
  106.1 21.7 %copy-start.6 = (bf16[2048,1024]{1,0:T(8,128)(2,1)S(1)}, bf16[2048,1024]{1,0:T(8,128)(2,1)}, u32[]{:S(2)}) copy-start(bf16[2048,1024]{1,0:T(8,128)(2,1)} %copy-done.5) | copy-start | bytes 12582916
  149.5 10.1 %copy-start.11 = (bf16[2,64,1536]{2,1,0:T(8,128)(2,1)S(1)}, bf16[2,64,1536]{2,1,0:T(8,128)(2,1)}, u32[]{:S(2)}) copy-start(bf16[2,64,1536]{2,1,0:T(8,128)(2,1)} %copy-done.10) | copy-start | bytes 1179652

commit v2 on v1

v2 whole, which is shorter than its diff:
```python
import functools

import jax
import jax.numpy as jnp
from jax import lax
from jax.experimental import pallas as pl
from jax.experimental.pallas import tpu as pltpu
from jax.sharding import PartitionSpec as P

STEPS = 5
HIST = 3
MIB = 1024 * 1024
BF16 = jnp.bfloat16
F32 = jnp.float32
ANY_SPEC = pl.BlockSpec(memory_space=pl.ANY)
VMEM_SPEC = pl.BlockSpec(memory_space=pltpu.VMEM)


def nt_dot(left, right):
    return lax.dot_general(left, right, (((1,), (1,)), ((), ())), preferred_element_type=F32)


def params(limit, **more):
    return pltpu.CompilerParams(vmem_limit_bytes=limit * MIB, **more)


def cost(flops, touched):
    return pl.CostEstimate(flops=int(flops), bytes_accessed=int(touched), transcendentals=0)


def history_kernel(history_ref, proj_ref, out_ref, held_ref, basis_ref, sems):
    slots, clusters, excite, unknowns = held_ref.shape
    copies = []
    for c in range(clusters):
        copies.append((
            pltpu.make_async_copy(proj_ref.at[c], basis_ref.at[c], sems.at[c, slots]),
            [pltpu.make_async_copy(history_ref.at[h, c], held_ref.at[h, c], sems.at[c, h]) for h in range(slots)],
        ))
    for basis, parts in copies:
        for part in parts:
            part.start()
        basis.start()
    sides = []
    for c, (basis, parts) in enumerate(copies):
        for part in parts:
            part.wait()
        basis.wait()
        left = jnp.concatenate([held_ref[h, c] for h in range(slots)], axis=0)
        sides.append(nt_dot(left, basis_ref[c]))
    both = jnp.concatenate(sides, axis=1).astype(BF16)
    for h in range(slots):
        out_ref[h] = both[h * excite:(h + 1) * excite]


def project_history(history, proj_basis):
    slots, clusters, excite, unknowns = history.shape
    rank = proj_basis.shape[1]
    return pl.pallas_call(
        history_kernel,
        out_shape=jax.ShapeDtypeStruct((slots, excite, clusters * rank), BF16),
        in_specs=[ANY_SPEC] * 2,
        out_specs=VMEM_SPEC,
        scratch_shapes=[
            pltpu.VMEM(history.shape, BF16),
            pltpu.VMEM(proj_basis.shape, BF16),
            pltpu.SemaphoreType.DMA((clusters, slots + 1)),
        ],
        compiler_params=params(8),
        name="project_history",
    )(in_hbm(history), in_hbm(proj_basis))


def order_kernel(stride, own_ref, by1_ref, by3_ref, by2_ref, out_ref):
    me = lax.rem(lax.axis_index("src") // stride, 4)
    for k, ref in ((0, own_ref), (1, by1_ref), (3, by3_ref), (2, by2_ref)):
        out_ref[me ^ k] = ref[...]


def exchange(array, stride, name):
    arrived = [
        lax.ppermute(array, "src", [(i, i ^ (k * stride)) for i in range(16)]) for k in (1, 3, 2)
    ]
    return pl.pallas_call(
        functools.partial(order_kernel, stride),
        out_shape=jax.ShapeDtypeStruct((4,) + array.shape, array.dtype),
        in_specs=[VMEM_SPEC] * 4,
        out_specs=VMEM_SPEC,
        compiler_params=params(8),
        name=name,
    )(array, *arrived)


def near_kernel(depth, incident_ref, expand_ref, near_ref, proj_ref,
                incoming_ref, expanded_ref, start_ref, transfer_ref,
                held_ref, tiles_ref, basis_ref, held_sems, tile_sems, basis_sems):
    steps, clusters, excite, unknowns = incident_ref.shape
    rank = expand_ref.shape[1]
    count, _, tile = tiles_ref.shape
    per = count // clusters
    head = steps * excite

    def held_copy(c):
        return [
            pltpu.make_async_copy(
                incident_ref.at[t, c], held_ref.at[c, pl.ds(t * excite, excite)], held_sems.at[c, t])
            for t in range(steps)
        ] + [pltpu.make_async_copy(expand_ref.at[c], held_ref.at[c, pl.ds(head, rank)], held_sems.at[c, steps])]

    def tile_copy(i):
        c, n = divmod(i, per)
        return pltpu.make_async_copy(near_ref.at[c, :, pl.ds(n * tile, tile)], tiles_ref.at[i], tile_sems.at[i])

    def basis_copy(c):
        return pltpu.make_async_copy(proj_ref.at[c], basis_ref.at[c], basis_sems.at[c])

    def fetch(i):
        if i < count:
            c, n = divmod(i, per)
            if n == 0:
                for copy in held_copy(c):
                    copy.start()
            tile_copy(i).start()
            if n == 0:
                basis_copy(c).start()

    for i in range(depth):
        fetch(i)
    small = []
    for c in range(clusters):
        for copy in held_copy(c):
            copy.wait()
        total = None
        for n in range(per):
            tile_copy(c * per + n).wait()
            fetch(c * per + n + depth)
            if n == 0:
                basis_copy(c).wait()
            lanes = slice(n * tile, (n + 1) * tile)
            product = jnp.dot(held_ref[c], tiles_ref[c * per + n], preferred_element_type=F32).astype(BF16)
            for t in range(steps):
                incoming_ref[t, c, :, lanes] = product[t * excite:(t + 1) * excite]
            expanded_ref[c, :, lanes] = product[head:]
            part = nt_dot(product, basis_ref[c, :, lanes])
            total = part if total is None else total + part
        small.append(total)
    for t in range(steps):
        rows = slice(t * excite, (t + 1) * excite)
        start_ref[t] = jnp.concatenate([part[rows] for part in small], axis=1)
    zero = jnp.zeros((rank, rank), F32)
    full = jnp.concatenate([
        jnp.concatenate([small[0][head:], zero], axis=1),
        jnp.concatenate([zero, small[1][head:]], axis=1),
    ], axis=0)
    high = full.astype(BF16)
    low = (full - high.astype(F32)).astype(BF16)
    transfer_ref[...] = jnp.concatenate([high, low], axis=0)


def prepare_near(incident, expand_basis, near_inverse, proj_basis, tile=512, depth=2):
    steps, clusters, excite, unknowns = incident.shape
    rank = proj_basis.shape[1]
    rows = steps * excite + rank
    tiles = clusters * unknowns // tile
    return pl.pallas_call(
        functools.partial(near_kernel, depth),
        out_shape=(
            jax.ShapeDtypeStruct((steps, clusters, excite, unknowns), BF16),
            jax.ShapeDtypeStruct((clusters, rank, unknowns), BF16),
            jax.ShapeDtypeStruct((steps, excite, clusters * rank), F32),
            jax.ShapeDtypeStruct((2 * clusters * rank, clusters * rank), BF16),
        ),
        in_specs=[ANY_SPEC] * 4,
        out_specs=[VMEM_SPEC] * 4,
        scratch_shapes=[
            pltpu.VMEM((clusters, rows, unknowns), BF16),
            pltpu.VMEM((tiles, unknowns, tile), BF16),
            pltpu.VMEM((clusters, rank, unknowns), BF16),
            pltpu.SemaphoreType.DMA((clusters, steps + 1)),
            pltpu.SemaphoreType.DMA((tiles,)),
            pltpu.SemaphoreType.DMA((clusters,)),
        ],
        compiler_params=params(24),
        cost_estimate=cost(2 * clusters * rows * unknowns * (unknowns + rank), 2 * clusters * unknowns * unknowns),
        name="prepare_near",
    )(*[in_hbm(x) for x in (incident, expand_basis, near_inverse, proj_basis)])


def build_kernel(depth, couplings_ref, lags_ref, w1_ref, w2_ref, w3_ref, held_ref, sems):
    taps, _, columns_here = couplings_ref.shape
    clusters, columns = lags_ref.shape
    rank = w1_ref.shape[0] // clusters
    blocks = columns // columns_here
    rows_in = 256
    group = rows_in // blocks
    pieces, part = held_ref.shape[0], held_ref.shape[2]
    clusters_here = clusters // pieces

    def piece_copy(i, p):
        return pltpu.make_async_copy(
            couplings_ref.at[p, pl.ds(i * part, part)], held_ref.at[i, p], sems.at[i, p])

    def fetch(i):
        if i < pieces:
            for p in range(taps):
                piece_copy(i, p).start()

    for i in range(depth):
        fetch(i)
    to = lax.broadcasted_iota(jnp.int32, (rows_in, rows_in), 0)
    source = lax.broadcasted_iota(jnp.int32, (rows_in, rows_in), 1)
    wanted = (to % group) * blocks + to // group
    perm = jnp.where(source == wanted, 1.0, 0.0).astype(BF16)

    for i in range(pieces):
        for p in range(taps):
            piece_copy(i, p).wait()
        fetch(i + depth)
        for j in range(clusters_here):
            cluster = i * clusters_here + j
            lag = lags_ref[cluster:cluster + 1, :]
            masks = []
            for delay in (1.0, 2.0):
                row = jnp.where(lag == delay, 1.0, 0.0)
                masks.append([
                    jnp.broadcast_to(row[:, o * 128:(o + 1) * 128], (group, 128)).astype(BF16)
                    for o in range(blocks)
                ])
            for g in range(rank // group):
                at = j * (rank * blocks) + g * rows_in
                pair = jnp.concatenate([held_ref[i, p, at:at + rows_in, :] for p in range(taps)], axis=1)
                ordered = jnp.dot(perm, pair, preferred_element_type=F32).astype(BF16)
                out = slice(cluster * rank + g * group, cluster * rank + (g + 1) * group)
                for o in range(blocks):
                    k0 = ordered[o * group:(o + 1) * group, :128]
                    k1 = ordered[o * group:(o + 1) * group, 128:]
                    m1, m2 = masks[0][o], masks[1][o]
                    lanes = slice(o * 128, (o + 1) * 128)
                    w1_ref[out, lanes] = k0 * m1
                    w2_ref[out, lanes] = k0 * m2 + k1 * m1
                    w3_ref[out, lanes] = k1 * m2


def build_matrices(couplings, lag_rows, pieces=4, depth=2):
    clusters, columns = lag_rows.shape
    taps, count, width = couplings.shape
    rows = count * width // columns
    return pl.pallas_call(
        functools.partial(build_kernel, depth),
        out_shape=[jax.ShapeDtypeStruct((rows, columns), BF16)] * 3,
        in_specs=[ANY_SPEC, VMEM_SPEC],
        out_specs=[VMEM_SPEC] * 3,
        scratch_shapes=[
            pltpu.VMEM((pieces, taps, count // pieces, width), BF16),
            pltpu.SemaphoreType.DMA((pieces, taps)),
        ],
        compiler_params=params(28),
        cost_estimate=cost(2 * taps * 256 * rows * columns, 10 * rows * columns),
        name="build_matrices",
    )(in_hbm(couplings), lag_rows)


def in_hbm(array):
    return pltpu.with_memory_space_constraint(array, pltpu.HBM)


def wide(gathered_ref):
    return jnp.concatenate([gathered_ref[s] for s in range(gathered_ref.shape[0])], axis=1)


def send_field(field_ref, total):
    for o in range(field_ref.shape[0]):
        field_ref[o] = total[:, o * 128:(o + 1) * 128].astype(BF16)


def step0_kernel(history_ref, transfer_ref, w1_ref, w2_ref, w3_ref, field_ref, base_ref):
    excite = base_ref.shape[1]
    old, middle, new = [
        jnp.concatenate([history_ref[y, x, h] for y in range(4) for x in range(4)], axis=1)
        for h in range(HIST)
    ]
    one = jnp.dot(new, w1_ref[...], preferred_element_type=F32)
    two = jnp.dot(jnp.concatenate([middle, new], axis=0), w2_ref[...], preferred_element_type=F32)
    three = jnp.dot(jnp.concatenate([old, middle, new], axis=0), w3_ref[...], preferred_element_type=F32)
    send_field(field_ref, one + two[:excite] + three[:excite])
    base_ref[0] = two[excite:] + three[excite:2 * excite]
    base_ref[1] = three[2 * excite:]


def step1_kernel(q0_ref, base_ref, w1_ref, field_ref):
    send_field(field_ref, base_ref[0] + jnp.dot(wide(q0_ref), w1_ref[...], preferred_element_type=F32))


def step2_kernel(q0_ref, q1_ref, base_ref, w1_ref, w2_ref, field_ref, next_ref):
    excite = base_ref.shape[1]
    one, zero = wide(q1_ref), wide(q0_ref)
    two = jnp.dot(jnp.concatenate([zero, one], axis=0), w2_ref[...], preferred_element_type=F32)
    send_field(field_ref, base_ref[1] + two[:excite] + jnp.dot(one, w1_ref[...], preferred_element_type=F32))
    next_ref[...] = two[excite:]


def step3_kernel(q0_ref, q1_ref, q2_ref, base_ref, w1_ref, w3_ref, field_ref, next_ref):
    excite = base_ref.shape[0]
    three = jnp.dot(jnp.concatenate([wide(q0_ref), wide(q1_ref)], axis=0), w3_ref[...], preferred_element_type=F32)
    send_field(field_ref, base_ref[...] + three[:excite]
               + jnp.dot(wide(q2_ref), w1_ref[...], preferred_element_type=F32))
    next_ref[...] = three[excite:]


def step4_kernel(q2_ref, q3_ref, base_ref, w1_ref, w2_ref, field_ref):
    send_field(field_ref, base_ref[...]
               + jnp.dot(wide(q2_ref), w2_ref[...], preferred_element_type=F32)
               + jnp.dot(wide(q3_ref), w1_ref[...], preferred_element_type=F32))


def couple(kernel, name, blocks, extra, gathered, bases, weights):
    excite, width = gathered[0].shape[-2:]
    shapes = [jax.ShapeDtypeStruct((blocks, excite, width), BF16)]
    if extra:
        shapes.append(jax.ShapeDtypeStruct(extra, F32))
    got = pl.pallas_call(
        kernel,
        out_shape=shapes,
        in_specs=[VMEM_SPEC] * (len(gathered) + len(bases) + len(weights)),
        out_specs=[VMEM_SPEC] * len(shapes),
        compiler_params=params(16),
        name=name,
    )(*gathered, *bases, *weights)
    return got if extra else got[0]


def project_kernel(parts_ref, start_ref, transfer_ref, field_ref, out_ref):
    total = parts_ref[0].astype(F32)
    for o in range(1, parts_ref.shape[0]):
        total = total + parts_ref[o].astype(F32)
    field = total.astype(BF16)
    field_ref[...] = field
    q = start_ref[0] - jnp.dot(
        jnp.concatenate([field, field], axis=1), transfer_ref[...], preferred_element_type=F32)
    q = q.astype(BF16)
    for s in range(out_ref.shape[0]):
        out_ref[s] = q


def project_step(parts, start, transfer, copies, step):
    blocks, excite, width = parts.shape
    return pl.pallas_call(
        project_kernel,
        grid=(1,),
        out_shape=(
            jax.ShapeDtypeStruct((excite, width), BF16),
            jax.ShapeDtypeStruct((copies, excite, width), BF16),
        ),
        in_specs=[
            pl.BlockSpec(parts.shape, lambda i: (0, 0, 0)),
            pl.BlockSpec((1, excite, width), lambda i: (step, 0, 0)),
            pl.BlockSpec(transfer.shape, lambda i: (0, 0)),
        ],
        out_specs=(
            pl.BlockSpec((excite, width), lambda i: (0, 0)),
            pl.BlockSpec((copies, excite, width), lambda i: (0, 0, 0)),
        ),
        compiler_params=params(8),
        name="project_step",
    )(parts, start, transfer)


def currents_kernel(incoming_ref, expanded_ref, parts_ref, f0_ref, f1_ref, f2_ref, f3_ref, out_ref):
    total = parts_ref[0].astype(F32)
    for o in range(1, parts_ref.shape[0]):
        total = total + parts_ref[o].astype(F32)
    fields = [f0_ref[...], f1_ref[...], f2_ref[...], f3_ref[...], total.astype(BF16)]
    excite = out_ref.shape[2]
    rank = expanded_ref.shape[1]
    for c in range(out_ref.shape[1]):
        left = jnp.concatenate([f[:, c * rank:(c + 1) * rank] for f in fields], axis=0)
        far = jnp.dot(left, expanded_ref[c], preferred_element_type=F32)
        for t in range(out_ref.shape[0]):
            out_ref[t, c] = (incoming_ref[t, c].astype(F32) - far[t * excite:(t + 1) * excite]).astype(BF16)


def final_currents(incoming, expanded, parts, fields, tile=512):
    steps, clusters, excite, unknowns = incoming.shape
    rank = expanded.shape[1]
    small = pl.BlockSpec(fields[0].shape, lambda n: (0, 0))
    return pl.pallas_call(
        currents_kernel,
        grid=(unknowns // tile,),
        out_shape=jax.ShapeDtypeStruct(incoming.shape, BF16),
        in_specs=[
            pl.BlockSpec((steps, clusters, excite, tile), lambda n: (0, 0, 0, n)),
            pl.BlockSpec((clusters, rank, tile), lambda n: (0, 0, n)),
            pl.BlockSpec(parts.shape, lambda n: (0, 0, 0)),
        ] + [small] * len(fields),
        out_specs=pl.BlockSpec((steps, clusters, excite, tile), lambda n: (0, 0, 0, n)),
        compiler_params=params(16),
        name="final_currents",
    )(incoming, expanded, parts, *fields)


def per_device(history, incident, proj_basis, expand_basis, near_inverse, couplings, lags):
    clusters, rank, unknowns = proj_basis.shape
    width = clusters * rank
    taps, src_rows, blocks = couplings.shape[:3]
    src_clusters = lags.shape[0]
    senders = src_rows // width
    flat = couplings.reshape(taps, src_rows * blocks, width)
    spread = jnp.repeat(jnp.eye(blocks * clusters, dtype=F32), rank, axis=1)
    lag_rows = jnp.dot(lags.reshape(src_clusters, blocks * clusters).astype(F32), spread)

    def gather(copies):
        return lax.all_to_all(copies, "src", 0, 0)

    def scatter(chunks):
        return lax.all_to_all(chunks, "obs", 0, 0)

    mine = project_history(history, proj_basis)
    gathered = exchange(exchange(mine, 1, "order_x"), 4, "order_y")
    incoming, expanded, start, transfer = prepare_near(incident, expand_basis, near_inverse, proj_basis)
    w1, w2, w3 = build_matrices(flat, lag_rows)
    fields, past = [], []
    excite = history.shape[2]
    full = (excite, blocks * width)
    ahead = None
    for step in range(STEPS):
        if step == 0:
            chunks, base = couple(step0_kernel, "step0", blocks, (2,) + full, [gathered], [transfer], [w1, w2, w3])
        elif step == 1:
            chunks = couple(step1_kernel, "step1", blocks, None, past, [base], [w1])
        elif step == 2:
            chunks, ahead = couple(step2_kernel, "step2", blocks, full, past, [base], [w1, w2])
        elif step == 3:
            chunks, ahead = couple(step3_kernel, "step3", blocks, full, past, [ahead], [w1, w3])
        else:
            chunks = couple(step4_kernel, "step4", blocks, None, past[2:], [ahead], [w1, w2])
        parts = scatter(chunks)
        if step + 1 < STEPS:
            field, copies = project_step(parts, start, transfer, senders, step)
            fields.append(field)
            past.append(gather(copies))
    return final_currents(incoming, expanded, parts, fields)


def solution(mesh):
    placed = (
        P(None, ("obs", "src"), None, None),
        P(None, ("obs", "src"), None, None),
        P(("obs", "src"), None, None),
        P(("obs", "src"), None, None),
        P(("obs", "src"), None, None),
        P(None, "obs", None, "src", None),
        P("obs", None, "src", None),
    )
    return jax.shard_map(
        per_device,
        mesh=mesh,
        in_specs=placed,
        out_specs=P(None, ("obs", "src"), None, None),
        check_vma=False,
    )
```

time: 163 us -> 135 us (0.83)
  local copies, waits for them, and re-layouts: 21.9 us -> 0.21 us
  blocking collectives: 83.1 us -> 95.3 us
  waiting for transfers between devices: 13.4 us -> 2.34 us
  Pallas kernels: 30.1 us -> 26.2 us
  starting transfers between devices: 12.4 us -> 8.66 us
    unnamed x30 -> x0, local copies, waits for them, and re-layouts: 21.7 us -> none
    all_to_all x2 -> x0, waiting for transfers between devices: 13.4 us -> none  [the longest x1 13.4 us: gather(): return lax.all_to_all(copies, 'src', 0, 0)]
    all_to_all x2 -> x0, starting transfers between devices: 12.4 us -> none  [the longest x1 7.12 us: gather(): return lax.all_to_all(copies, 'src', 0, 0)]
    all_to_all x4 -> x5, blocking collectives: 36.1 us -> 45.3 us  [scatter(): return lax.all_to_all(chunks, 'obs', 0, 0)]
    ppermute x0 -> x6, starting transfers between devices: none -> 8.66 us  [exchange(): lax.ppermute(array, 'src', [(i, i ^ k * stride) for i in range(16)])]
    pallas_call x7 -> x10, Pallas kernels: 27.1 us -> 23.2 us  [the longest x1 7.85 us: prepare_near(): pl.pallas_call(functools.partial(near_kernel, depth), out_shape=(jax.Shap...]
    all_to_all x4, blocking collectives: 47 us -> 50 us  [gather(): return lax.all_to_all(copies, 'src', 0, 0)]
    ppermute x0 -> x6, waiting for transfers between devices: none -> 2.34 us  [exchange(): lax.ppermute(array, 'src', [(i, i ^ k * stride) for i in range(16)])]
  transfers between devices with their start and end apart: 2 -> 6, of which waited for: 1 -> 2; matrix products, arithmetic and copies ran while one was open for 1% -> 1% of each run, Pallas kernels for 5% -> 10%
where the time goes in v2:
time: 135 us; the launch traced here: 134 us
  blocking collectives  95.3 us (71%)
  Pallas kernels  26.2 us (19%)
  starting transfers between devices  8.66 us (6%)
  waiting for transfers between devices  2.34 us (2%)
    all_to_all x4, blocking collectives, gather(): return lax.all_to_all(copies, 'src', 0, 0)  50 us
    all_to_all x5, blocking collectives, scatter(): return lax.all_to_all(chunks, 'obs', 0, 0)  45.3 us
    ppermute x6, starting transfers between devices, exchange(): lax.ppermute(array, 'src', [(i, i ^ k * stride) for i in range(16)])  8.66 us
    pallas_call x1, Pallas kernels, prepare_near(): pl.pallas_call(functools.partial(near_kernel, depth), out_shape=(jax.Shap...  7.85 us
    pallas_call x5, Pallas kernels, couple(): pl.pallas_call(kernel, out_shape=shapes, in_specs=[VMEM_SPEC] * (len(gath...  7.41 us
    pallas_call x1, Pallas kernels, build_matrices(): pl.pallas_call(functools.partial(build_kernel, depth), out_shape=[jax.Sha...  5.57 us
  transfers between devices with their start and end apart: 6, of which 2 were waited for; matrix products, arithmetic and copies ran while one was open for 1% of the time, Pallas kernels for 10%

profile of v2, /device:TPU:0, one launch (start us, length us, event | category | flops | bytes accessed | tf_op | source)
XLA Modules:
  0.0 133.8 jit_solution(384414799786285540)
XLA Ops:
  0.0 2.2 %project_history.1.own_ref = bf16[3,64,128]{2,1,0:T(8,128)(2,1)S(1)} custom-call(bf16[3,2,64,1536]{3,2,1,0:T(8,128)(2,1)} %history_ref.1, bf16[2,64,1536]{2,1,0:T(8,128)(2,1)} %proj_ref.3), custom_call_target="tpu_custom_call" | custom-call | tf_op jit(solution)/shard_map/project_history/pallas_call | solution.py:58
  2.2 3.2 %collective-permute-start.2 = (bf16[3,64,128]{2,1,0:T(8,128)(2,1)S(1)}, bf16[3,64,128]{2,1,0:T(8,128)(2,1)S(1)}, u32[]{:S(2)}, u32[]{:S(2)}) collective-permute-start(bf16[3,64,128]{2,1,0:T(8,128)(2,1)S(1)} %project_history.1.own_ref), channel_id=1, source_target_pairs={{0,2},{1,3},{2,0},{3,1},{4,6},{5,7},{6,4},{7,5},{8,10},{9,11},{10,... | collective-permute-start | bytes 147464 | tf_op jit(solution)/shard_map/ppermute | solution.py:81
  5.4 1.1 collective-permute-start.1
  6.6 0.0 collective-permute-start
  6.6 0.7 convert_element_type.10
  7.3 0.1 broadcast_in_dim.3
  7.4 0.1 reshape.9
  7.5 7.9 %prepare_near.1 = (bf16[5,2,64,1536]{3,2,1,0:T(8,128)(2,1)S(1)}, bf16[2,64,1536]{2,1,0:T(8,128)(2,1)S(1)}, f32[5,64,128]{2,1,0:T(8,128)S(1)}, bf16[256,128]{1,0:T(8,128)(2,1)S(1)}) custom-call(bf16[5,2,64,1536]{3,2,1,0:T(8,128)(2,1)} %incident_ref.1, bf16[2,64,1536]{2,1,0:T(8,128)(2,1)} %expand_ref.1, bf16[2,1536,1536]{2,1,0:T(8,128)(2,1)} %near_ref.1, ...), custom_call_target="tpu_custom_call" | custom-call | flops 3774873600 | bytes 9437184 | tf_op jit(solution)/shard_map/prepare_near/pallas_call | solution.py:164
  15.4 0.2 convolution_bitcast_fusion.lags_ref
  15.6 0.0 collective-permute-done.2.by2_ref
  15.6 0.0 collective-permute-done.1.by3_ref
  15.6 0.0 collective-permute-done.by1_ref
  15.6 3.3 %collective-permute-start.5 = (bf16[4,3,64,128]{3,2,1,0:T(8,128)(2,1)S(1)}, bf16[4,3,64,128]{3,2,1,0:T(8,128)(2,1)S(1)}, u32[]{:S(2)}, u32[]{:S(2)}) collective-permute-start(bf16[4,3,64,128]{3,2,1,0:T(8,128)(2,1)S(1)} %order_x.1.own_ref), channel_id=1, source_target_pairs={{0,8},{1,9},{2,10},{3,11},{4,12},{5,13},{6,14},{7,15},{8,0},{9,1},... | collective-permute-start | bytes 589832 | tf_op jit(solution)/shard_map/ppermute | solution.py:81
  18.9 1.1 collective-permute-start.4
  20.0 0.0 collective-permute-start.3
  20.0 5.6 %build_matrices.1 = (bf16[2048,1024]{1,0:T(8,128)(2,1)S(1)}, bf16[2048,1024]{1,0:T(8,128)(2,1)S(1)}, bf16[2048,1024]{1,0:T(8,128)(2,1)S(1)}) custom-call(bf16[2,16384,128]{2,1,0:T(8,128)(2,1)} %bitcast.6, f32[32,1024]{1,0:T(8,128)S(1)} %convolution_bitcast_fusion.lags_ref), custom_call_target="tpu_custom_call" | custom-call | flops 2147483648 | bytes 20971520 | tf_op jit(solution)/shard_map/build_matrices/pallas_call | solution.py:247
  25.5 0.0 collective-permute-done.5.by2_ref
  25.5 2.0 %collective-permute-done.4.by3_ref = bf16[4,3,64,128]{3,2,1,0:T(8,128)(2,1)S(1)} collective-permute-done((bf16[4,3,64,128]{3,2,1,0:T(8,128)(2,1)S(1)}, bf16[4,3,64,128]{3,2,1,0:T(8,128)(2,1)S(1)}, u32[]{:S(2)}, u32[]{:S(2)}) %collective-permute-start.4) | collective-permute-done | bytes 196640 | tf_op jit(solution)/shard_map/ppermute | solution.py:81
  27.5 0.4 collective-permute-done.3.by1_ref
  27.9 0.1 order_y.1.history_ref
  28.0 2.2 %step0.1 = (bf16[8,64,128]{2,1,0:T(8,128)(2,1)S(1)}, f32[2,64,1024]{2,1,0:T(8,128)S(1)}) custom-call(bf16[4,4,3,64,128]{4,3,2,1,0:T(8,128)(2,1)S(1)} %order_y.1.history_ref, bf16[256,128]{1,0:T(8,128)(2,1)S(1)} %get-tuple-element.28.transfer_ref, bf16[2048,1024]{1,0:T(8,128)(2,1)S(1)} %get-tuple-element.29.w1_ref, ...), custom_call_target="tpu_custom_call" | custom-call | tf_op jit(solution)/shard_map/step0/pallas_call | solution.py:320
  30.2 11.2 %all_to_all.45.parts_ref = bf16[8,64,128]{2,1,0:T(8,128)(2,1)S(1)} all-to-all(bf16[8,64,128]{2,1,0:T(8,128)(2,1)S(1)} %get-tuple-element.32), channel_id=1, replica_groups=mesh['obs'=8,'src'=16] {'obs'}, dimensions={0} | all-to-all | bytes 262144 | tf_op jit(solution)/shard_map/all_to_all | solution.py:414
  41.4 0.2 project_step.4
  41.6 15.2 %all_to_all.46.q0_ref = bf16[16,64,128]{2,1,0:T(8,128)(2,1)S(1)} all-to-all(bf16[16,64,128]{2,1,0:T(8,128)(2,1)S(1)} %get-tuple-element.34), channel_id=1, replica_groups=mesh['obs'=8,'src'=16] {'src'}, dimensions={0} | all-to-all | bytes 524288 | tf_op jit(solution)/shard_map/all_to_all | solution.py:411
  56.8 0.8 step1.1
  57.7 8.5 %all_to_all.47.parts_ref = bf16[8,64,128]{2,1,0:T(8,128)(2,1)S(1)} all-to-all(bf16[8,64,128]{2,1,0:T(8,128)(2,1)S(1)} %step1.1), channel_id=1, replica_groups=mesh['obs'=8,'src'=16] {'obs'}, dimensions={0} | all-to-all | bytes 262144 | tf_op jit(solution)/shard_map/all_to_all | solution.py:414
  66.2 0.2 project_step.5
  66.3 11.6 %all_to_all.48.q1_ref = bf16[16,64,128]{2,1,0:T(8,128)(2,1)S(1)} all-to-all(bf16[16,64,128]{2,1,0:T(8,128)(2,1)S(1)} %get-tuple-element.36), channel_id=1, replica_groups=mesh['obs'=8,'src'=16] {'src'}, dimensions={0} | all-to-all | bytes 524288 | tf_op jit(solution)/shard_map/all_to_all | solution.py:411
  77.9 1.4 %step2.1 = (bf16[8,64,128]{2,1,0:T(8,128)(2,1)S(1)}, f32[64,1024]{1,0:T(8,128)S(1)}) custom-call(bf16[16,64,128]{2,1,0:T(8,128)(2,1)S(1)} %all_to_all.46.q0_ref, bf16[16,64,128]{2,1,0:T(8,128)(2,1)S(1)} %all_to_all.48.q1_ref, f32[2,64,1024]{2,1,0:T(8,128)S(1)} %get-tuple-element.35.base_ref, bf16[2048,1024]{1,0:T(8,128)(2,1)S(1)} %get-tuple-element.29.w1_ref, ...), custom_call_target="tpu_custom_call" | custom-call | tf_op jit(solution)/shard_map/step2/pallas_call | solution.py:320
  79.3 8.5 %all_to_all.49.parts_ref = bf16[8,64,128]{2,1,0:T(8,128)(2,1)S(1)} all-to-all(bf16[8,64,128]{2,1,0:T(8,128)(2,1)S(1)} %get-tuple-element.37), channel_id=1, replica_groups=mesh['obs'=8,'src'=16] {'obs'}, dimensions={0} | all-to-all | bytes 262144 | tf_op jit(solution)/shard_map/all_to_all | solution.py:414
  87.9 0.2 project_step.6
  88.0 11.6 %all_to_all.50.q2_ref = bf16[16,64,128]{2,1,0:T(8,128)(2,1)S(1)} all-to-all(bf16[16,64,128]{2,1,0:T(8,128)(2,1)S(1)} %get-tuple-element.38), channel_id=1, replica_groups=mesh['obs'=8,'src'=16] {'src'}, dimensions={0} | all-to-all | bytes 524288 | tf_op jit(solution)/shard_map/all_to_all | solution.py:411
  99.6 1.4 %step3.1 = (bf16[8,64,128]{2,1,0:T(8,128)(2,1)S(1)}, f32[64,1024]{1,0:T(8,128)S(1)}) custom-call(bf16[16,64,128]{2,1,0:T(8,128)(2,1)S(1)} %all_to_all.46.q0_ref, bf16[16,64,128]{2,1,0:T(8,128)(2,1)S(1)} %all_to_all.48.q1_ref, bf16[16,64,128]{2,1,0:T(8,128)(2,1)S(1)} %all_to_all.50.q2_ref, f32[64,1024]{1,0:T(8,128)S(1)} %get-tuple-element.39.base_ref, ...), custom_call_target="tpu_custom_call" | custom-call | tf_op jit(solution)/shard_map/step3/pallas_call | solution.py:320
  101.0 8.5 %all_to_all.51.parts_ref = bf16[8,64,128]{2,1,0:T(8,128)(2,1)S(1)} all-to-all(bf16[8,64,128]{2,1,0:T(8,128)(2,1)S(1)} %get-tuple-element.40), channel_id=1, replica_groups=mesh['obs'=8,'src'=16] {'obs'}, dimensions={0} | all-to-all | bytes 262144 | tf_op jit(solution)/shard_map/all_to_all | solution.py:414
  109.5 0.2 project_step.7
  109.7 11.6 %all_to_all.52.q3_ref = bf16[16,64,128]{2,1,0:T(8,128)(2,1)S(1)} all-to-all(bf16[16,64,128]{2,1,0:T(8,128)(2,1)S(1)} %get-tuple-element.41), channel_id=1, replica_groups=mesh['obs'=8,'src'=16] {'src'}, dimensions={0} | all-to-all | bytes 524288 | tf_op jit(solution)/shard_map/all_to_all | solution.py:411
  121.3 1.6 %step4.1 = bf16[8,64,128]{2,1,0:T(8,128)(2,1)S(1)} custom-call(bf16[16,64,128]{2,1,0:T(8,128)(2,1)S(1)} %all_to_all.50.q2_ref, bf16[16,64,128]{2,1,0:T(8,128)(2,1)S(1)} %all_to_all.52.q3_ref, f32[64,1024]{1,0:T(8,128)S(1)} %get-tuple-element.42.base_ref, bf16[2048,1024]{1,0:T(8,128)(2,1)S(1)} %get-tuple-element.29.w1_ref, ...), custom_call_target="tpu_custom_call" | custom-call | tf_op jit(solution)/shard_map/step4/pallas_call | solution.py:320
  122.9 8.5 %all_to_all.53.parts_ref = bf16[8,64,128]{2,1,0:T(8,128)(2,1)S(1)} all-to-all(bf16[8,64,128]{2,1,0:T(8,128)(2,1)S(1)} %step4.1), channel_id=1, replica_groups=mesh['obs'=8,'src'=16] {'obs'}, dimensions={0} | all-to-all | bytes 262144 | tf_op jit(solution)/shard_map/all_to_all | solution.py:414
  131.4 2.4 %final_currents.1 = bf16[5,2,64,1536]{3,2,1,0:T(8,128)(2,1)} custom-call(bf16[5,2,64,1536]{3,2,1,0:T(8,128)(2,1)S(1)} %get-tuple-element.26.incoming_ref, bf16[2,64,1536]{2,1,0:T(8,128)(2,1)S(1)} %get-tuple-element.27.expanded_ref, bf16[8,64,128]{2,1,0:T(8,128)(2,1)S(1)} %all_to_all.53.parts_ref, bf16[64,128]{1,0:T(8,128)(2,1)S(1)} %get-tuple-element.43.f0_ref, ...), custom_call_target="tpu_custom_call" | custom-call | tf_op jit(solution)/shard_map/final_currents/pallas_call | solution.py:385
  (2 shorter events, 0.0 us)
Async XLA Ops:
  2.2 13.3 %collective-permute-start.2 = (bf16[3,64,128]{2,1,0:T(8,128)(2,1)S(1)}, bf16[3,64,128]{2,1,0:T(8,128)(2,1)S(1)}, u32[]{:S(2)}, u32[]{:S(2)}) collective-permute-start(bf16[3,64,128]{2,1,0:T(8,128)(2,1)S(1)} %project_history.1.own_ref), channel_id=1, source_target_pairs={{0,2},{1,3},{2,0},{3,1},{4,6},{5,7},{6,4},{7,5},{8,10},{9,11},{10,... | collective-permute-start | bytes 147464 | tf_op jit(solution)/shard_map/ppermute | solution.py:81
  5.4 10.1 %collective-permute-start.1 = (bf16[3,64,128]{2,1,0:T(8,128)(2,1)S(1)}, bf16[3,64,128]{2,1,0:T(8,128)(2,1)S(1)}, u32[]{:S(2)}, u32[]{:S(2)}) collective-permute-start(bf16[3,64,128]{2,1,0:T(8,128)(2,1)S(1)} %project_history.1.own_ref), channel_id=1, source_target_pairs={{0,3},{1,2},{2,1},{3,0},{4,7},{5,6},{6,5},{7,4},{8,11},{9,10},{10,... | collective-permute-start | bytes 147464 | tf_op jit(solution)/shard_map/ppermute | solution.py:81
  6.6 9.0 %collective-permute-start = (bf16[3,64,128]{2,1,0:T(8,128)(2,1)S(1)}, bf16[3,64,128]{2,1,0:T(8,128)(2,1)S(1)}, u32[]{:S(2)}, u32[]{:S(2)}) collective-permute-start(bf16[3,64,128]{2,1,0:T(8,128)(2,1)S(1)} %project_history.1.own_ref), channel_id=1, source_target_pairs={{0,1},{1,0},{2,3},{3,2},{4,5},{5,4},{6,7},{7,6},{8,9},{9,8},{10,11... | collective-permute-start | bytes 147464 | tf_op jit(solution)/shard_map/ppermute | solution.py:81
  15.6 9.9 %collective-permute-start.5 = (bf16[4,3,64,128]{3,2,1,0:T(8,128)(2,1)S(1)}, bf16[4,3,64,128]{3,2,1,0:T(8,128)(2,1)S(1)}, u32[]{:S(2)}, u32[]{:S(2)}) collective-permute-start(bf16[4,3,64,128]{3,2,1,0:T(8,128)(2,1)S(1)} %order_x.1.own_ref), channel_id=1, source_target_pairs={{0,8},{1,9},{2,10},{3,11},{4,12},{5,13},{6,14},{7,15},{8,0},{9,1},... | collective-permute-start | bytes 589832 | tf_op jit(solution)/shard_map/ppermute | solution.py:81
  18.9 8.6 %collective-permute-start.4 = (bf16[4,3,64,128]{3,2,1,0:T(8,128)(2,1)S(1)}, bf16[4,3,64,128]{3,2,1,0:T(8,128)(2,1)S(1)}, u32[]{:S(2)}, u32[]{:S(2)}) collective-permute-start(bf16[4,3,64,128]{3,2,1,0:T(8,128)(2,1)S(1)} %order_x.1.own_ref), channel_id=1, source_target_pairs={{0,12},{1,13},{2,14},{3,15},{4,8},{5,9},{6,10},{7,11},{8,4},{9,5},... | collective-permute-start | bytes 589832 | tf_op jit(solution)/shard_map/ppermute | solution.py:81
  20.0 7.9 %collective-permute-start.3 = (bf16[4,3,64,128]{3,2,1,0:T(8,128)(2,1)S(1)}, bf16[4,3,64,128]{3,2,1,0:T(8,128)(2,1)S(1)}, u32[]{:S(2)}, u32[]{:S(2)}) collective-permute-start(bf16[4,3,64,128]{3,2,1,0:T(8,128)(2,1)S(1)} %order_x.1.own_ref), channel_id=1, source_target_pairs={{0,4},{1,5},{2,6},{3,7},{4,0},{5,1},{6,2},{7,3},{8,12},{9,13},{10,... | collective-permute-start | bytes 589832 | tf_op jit(solution)/shard_map/ppermute | solution.py:81

commit v3 on v2

v3 whole, which is shorter than its diff:
```python
import functools

import jax
import jax.numpy as jnp
from jax import lax
from jax.experimental import pallas as pl
from jax.experimental.pallas import tpu as pltpu
from jax.sharding import PartitionSpec as P

STEPS = 5
HIST = 3
TOP = 5
MIB = 1024 * 1024
BF16 = jnp.bfloat16
F32 = jnp.float32
ANY_SPEC = pl.BlockSpec(memory_space=pl.ANY)
VMEM_SPEC = pl.BlockSpec(memory_space=pltpu.VMEM)


def nt_dot(left, right):
    return lax.dot_general(left, right, (((1,), (1,)), ((), ())), preferred_element_type=F32)


def params(limit, **more):
    return pltpu.CompilerParams(vmem_limit_bytes=limit * MIB, **more)


def cost(flops, touched):
    return pl.CostEstimate(flops=int(flops), bytes_accessed=int(touched), transcendentals=0)


def history_kernel(history_ref, proj_ref, lags_ref, out_ref, spread_ref, held_ref, basis_ref, pairs_ref, sems, pairs_sem):
    slots, clusters, excite, unknowns = held_ref.shape
    blocks, observers, sources = lags_ref.shape
    columns = spread_ref.shape[1]
    pairs_copy = pltpu.make_async_copy(lags_ref, pairs_ref, pairs_sem)
    pairs_copy.start()
    copies = []
    for c in range(clusters):
        copies.append((
            pltpu.make_async_copy(proj_ref.at[c], basis_ref.at[c], sems.at[c, slots]),
            [pltpu.make_async_copy(history_ref.at[h, c], held_ref.at[h, c], sems.at[c, h]) for h in range(slots)],
        ))
    for basis, parts in copies:
        for part in parts:
            part.start()
        basis.start()
    pairs_copy.wait()
    pairs = jnp.concatenate([pairs_ref[o] for o in range(blocks)], axis=0).astype(F32)
    owner = lax.broadcasted_iota(jnp.int32, (blocks * observers, columns), 1) // (columns // (blocks * observers))
    row = lax.broadcasted_iota(jnp.int32, (blocks * observers, columns), 0)
    spread_ref[...] = lax.dot_general(
        pairs, jnp.where(owner == row, 1.0, 0.0), (((0,), (0,)), ((), ())), preferred_element_type=F32)
    sides = []
    for c, (basis, parts) in enumerate(copies):
        for part in parts:
            part.wait()
        basis.wait()
        left = jnp.concatenate([held_ref[h, c] for h in range(slots)], axis=0)
        sides.append(nt_dot(left, basis_ref[c]))
    both = jnp.concatenate(sides, axis=1).astype(BF16)
    for h in range(slots):
        out_ref[h] = both[h * excite:(h + 1) * excite]


def project_history(history, proj_basis, lags):
    slots, clusters, excite, unknowns = history.shape
    rank = proj_basis.shape[1]
    blocks, observers, sources = lags.shape
    return pl.pallas_call(
        history_kernel,
        out_shape=(
            jax.ShapeDtypeStruct((slots, excite, clusters * rank), BF16),
            jax.ShapeDtypeStruct((sources, blocks * observers * rank), F32),
        ),
        in_specs=[ANY_SPEC] * 3,
        out_specs=[VMEM_SPEC] * 2,
        scratch_shapes=[
            pltpu.VMEM(history.shape, BF16),
            pltpu.VMEM(proj_basis.shape, BF16),
            pltpu.VMEM(lags.shape, lags.dtype),
            pltpu.SemaphoreType.DMA((clusters, slots + 1)),
            pltpu.SemaphoreType.DMA,
        ],
        compiler_params=params(8),
        name="project_history",
    )(in_hbm(history), in_hbm(proj_basis), in_hbm(lags))


def order_kernel(stride, own_ref, by1_ref, by3_ref, by2_ref, after_ref, out_ref):
    me = lax.rem(lax.axis_index("src") // stride, 4)
    for k, ref in ((0, own_ref), (1, by1_ref), (3, by3_ref), (2, by2_ref)):
        out_ref[me ^ k] = ref[...]


def swap(array, stride):
    return [lax.ppermute(array, "src", [(i, i ^ (k * stride)) for i in range(16)]) for k in (1, 3, 2)]


def ordered(array, arrived, after, stride, name):
    return pl.pallas_call(
        functools.partial(order_kernel, stride),
        out_shape=jax.ShapeDtypeStruct((4,) + array.shape, array.dtype),
        in_specs=[VMEM_SPEC] * 4 + [ANY_SPEC],
        out_specs=VMEM_SPEC,
        compiler_params=params(8),
        name=name,
    )(array, *arrived, after)


def near_kernel(tile, incident_ref, expand_ref, near_ref, proj_ref, after_ref,
                incoming_ref, expanded_ref, start_ref, transfer_ref):
    steps, clusters, excite, unknowns = incident_ref.shape
    rank = expand_ref.shape[1]
    head = steps * excite
    small = []
    for c in range(clusters):
        left = jnp.concatenate([incident_ref[t, c] for t in range(steps)] + [expand_ref[c]], axis=0)
        total = None
        for n in range(unknowns // tile):
            lanes = slice(n * tile, (n + 1) * tile)
            product = jnp.dot(left, near_ref[c, :, lanes], preferred_element_type=F32).astype(BF16)
            for t in range(steps):
                incoming_ref[t, c, :, lanes] = product[t * excite:(t + 1) * excite]
            expanded_ref[c, :, lanes] = product[head:]
            part = nt_dot(product, proj_ref[c, :, lanes])
            total = part if total is None else total + part
        small.append(total)
    for t in range(steps):
        rows = slice(t * excite, (t + 1) * excite)
        start_ref[t] = jnp.concatenate([part[rows] for part in small], axis=1)
    zero = jnp.zeros((rank, rank), F32)
    full = jnp.concatenate([
        jnp.concatenate([small[0][head:], zero], axis=1),
        jnp.concatenate([zero, small[1][head:]], axis=1),
    ], axis=0)
    high = full.astype(BF16)
    low = (full - high.astype(F32)).astype(BF16)
    transfer_ref[...] = jnp.concatenate([high, low], axis=0)


def prepare_near(incident, expand_basis, near_inverse, proj_basis, after, tile=512):
    steps, clusters, excite, unknowns = incident.shape
    rank = proj_basis.shape[1]
    rows = steps * excite + rank
    return pl.pallas_call(
        functools.partial(near_kernel, tile),
        out_shape=(
            jax.ShapeDtypeStruct((steps, clusters, excite, unknowns), BF16),
            jax.ShapeDtypeStruct((clusters, rank, unknowns), BF16),
            jax.ShapeDtypeStruct((steps, excite, clusters * rank), F32),
            jax.ShapeDtypeStruct((2 * clusters * rank, clusters * rank), BF16),
        ),
        in_specs=[VMEM_SPEC] * 4 + [ANY_SPEC],
        out_specs=[VMEM_SPEC] * 4,
        compiler_params=params(20),
        cost_estimate=cost(2 * clusters * rows * unknowns * (unknowns + rank), 2 * clusters * unknowns * unknowns),
        name="prepare_near",
    )(incident, expand_basis, near_inverse, proj_basis, after)


def build_kernel(first, rank, depth, couplings_ref, spread_ref, after_ref, w1_ref, w2_ref, w3_ref, held_ref, sems):
    taps, _, columns_here = couplings_ref.shape
    columns = w1_ref.shape[1]
    blocks = columns // columns_here
    rows_in = 256
    group = rows_in // blocks
    pieces, part = held_ref.shape[0], held_ref.shape[2]
    clusters_here = part // (rank * blocks)

    def piece_copy(i, p):
        return pltpu.make_async_copy(
            couplings_ref.at[p, pl.ds(first * rank * blocks + i * part, part)], held_ref.at[i, p], sems.at[i, p])

    def fetch(i):
        if i < pieces:
            for p in range(taps):
                piece_copy(i, p).start()

    for i in range(depth):
        fetch(i)
    to = lax.broadcasted_iota(jnp.int32, (rows_in, rows_in), 0)
    source = lax.broadcasted_iota(jnp.int32, (rows_in, rows_in), 1)
    wanted = (to % group) * blocks + to // group
    perm = jnp.where(source == wanted, 1.0, 0.0).astype(BF16)

    for i in range(pieces):
        for p in range(taps):
            piece_copy(i, p).wait()
        fetch(i + depth)
        for j in range(clusters_here):
            cluster = i * clusters_here + j
            lag = spread_ref[first + cluster:first + cluster + 1, :]
            masks = []
            for delay in (1.0, 2.0):
                row = jnp.where(lag == delay, 1.0, 0.0)
                masks.append([
                    jnp.broadcast_to(row[:, o * 128:(o + 1) * 128], (group, 128)).astype(BF16)
                    for o in range(blocks)
                ])
            for g in range(rank // group):
                at = j * (rank * blocks) + g * rows_in
                pair = jnp.concatenate([held_ref[i, p, at:at + rows_in, :] for p in range(taps)], axis=1)
                ordered = jnp.dot(perm, pair, preferred_element_type=F32).astype(BF16)
                out = slice(cluster * rank + g * group, cluster * rank + (g + 1) * group)
                for o in range(blocks):
                    k0 = ordered[o * group:(o + 1) * group, :128]
                    k1 = ordered[o * group:(o + 1) * group, 128:]
                    m1, m2 = masks[0][o], masks[1][o]
                    lanes = slice(o * 128, (o + 1) * 128)
                    w1_ref[out, lanes] = k0 * m1
                    w2_ref[out, lanes] = k0 * m2 + k1 * m1
                    w3_ref[out, lanes] = k1 * m2


def build_matrices(first, pieces, couplings, spread, after, depth=3, clusters_here=4):
    sources, columns = spread.shape
    taps, count, width = couplings.shape
    blocks = columns // width
    rank = count // blocks // sources
    matrix = jax.ShapeDtypeStruct((pieces * clusters_here * rank, columns), BF16)
    return pl.pallas_call(
        functools.partial(build_kernel, first, rank, depth),
        out_shape=[matrix] * 3,
        in_specs=[ANY_SPEC, VMEM_SPEC, ANY_SPEC],
        out_specs=[VMEM_SPEC] * 3,
        scratch_shapes=[
            pltpu.VMEM((pieces, taps, clusters_here * rank * blocks, width), BF16),
            pltpu.SemaphoreType.DMA((pieces, taps)),
        ],
        compiler_params=params(20),
        cost_estimate=cost(6 * taps * 256 * matrix.size, 10 * matrix.size),
        name=f"build_matrices{first}",
    )(in_hbm(couplings), spread, after)


def in_hbm(array):
    return pltpu.with_memory_space_constraint(array, pltpu.HBM)


def wide(gathered_ref):
    return jnp.concatenate([gathered_ref[s] for s in range(gathered_ref.shape[0])], axis=1)


def send_field(field_ref, total):
    for o in range(field_ref.shape[0]):
        field_ref[o] = total[:, o * 128:(o + 1) * 128].astype(BF16)


def apply(left, top_ref, bottom_ref):
    half = top_ref.shape[0]
    return (jnp.dot(left[:, :half], top_ref[...], preferred_element_type=F32)
            + jnp.dot(left[:, half:], bottom_ref[...], preferred_element_type=F32))


def step0_kernel(history_ref, transfer_ref, w1a_ref, w1b_ref, w2a_ref, w2b_ref, w3a_ref, w3b_ref,
                 field_ref, base_ref):
    excite = base_ref.shape[1]
    old, middle, new = [
        jnp.concatenate([history_ref[y, x, h] for y in range(4) for x in range(4)], axis=1)
        for h in range(HIST)
    ]
    one = apply(new, w1a_ref, w1b_ref)
    two = apply(jnp.concatenate([middle, new], axis=0), w2a_ref, w2b_ref)
    three = apply(jnp.concatenate([old, middle, new], axis=0), w3a_ref, w3b_ref)
    send_field(field_ref, one + two[:excite] + three[:excite])
    base_ref[0] = two[excite:] + three[excite:2 * excite]
    base_ref[1] = three[2 * excite:]


def step1_kernel(q0_ref, base_ref, w1a_ref, w1b_ref, field_ref):
    send_field(field_ref, base_ref[0] + apply(wide(q0_ref), w1a_ref, w1b_ref))


def step2_kernel(q0_ref, q1_ref, base_ref, w1a_ref, w1b_ref, w2a_ref, w2b_ref, field_ref, next_ref):
    excite = base_ref.shape[1]
    one, zero = wide(q1_ref), wide(q0_ref)
    two = apply(jnp.concatenate([zero, one], axis=0), w2a_ref, w2b_ref)
    send_field(field_ref, base_ref[1] + two[:excite] + apply(one, w1a_ref, w1b_ref))
    next_ref[...] = two[excite:]


def step3_kernel(q0_ref, q1_ref, q2_ref, base_ref, w1a_ref, w1b_ref, w3a_ref, w3b_ref, field_ref, next_ref):
    excite = base_ref.shape[0]
    three = apply(jnp.concatenate([wide(q0_ref), wide(q1_ref)], axis=0), w3a_ref, w3b_ref)
    send_field(field_ref, base_ref[...] + three[:excite] + apply(wide(q2_ref), w1a_ref, w1b_ref))
    next_ref[...] = three[excite:]


def step4_kernel(q2_ref, q3_ref, base_ref, w1a_ref, w1b_ref, w2a_ref, w2b_ref, field_ref):
    send_field(field_ref, base_ref[...] + apply(wide(q2_ref), w2a_ref, w2b_ref)
               + apply(wide(q3_ref), w1a_ref, w1b_ref))


def couple(kernel, name, blocks, extra, gathered, bases, weights):
    excite, width = gathered[0].shape[-2:]
    shapes = [jax.ShapeDtypeStruct((blocks, excite, width), BF16)]
    if extra:
        shapes.append(jax.ShapeDtypeStruct(extra, F32))
    got = pl.pallas_call(
        kernel,
        out_shape=shapes,
        in_specs=[VMEM_SPEC] * (len(gathered) + len(bases) + len(weights)),
        out_specs=[VMEM_SPEC] * len(shapes),
        compiler_params=params(16),
        name=name,
    )(*gathered, *bases, *weights)
    return got if extra else got[0]


def project_kernel(parts_ref, start_ref, transfer_ref, field_ref, out_ref):
    total = parts_ref[0].astype(F32)
    for o in range(1, parts_ref.shape[0]):
        total = total + parts_ref[o].astype(F32)
    field = total.astype(BF16)
    field_ref[...] = field
    q = start_ref[0] - jnp.dot(
        jnp.concatenate([field, field], axis=1), transfer_ref[...], preferred_element_type=F32)
    q = q.astype(BF16)
    for s in range(out_ref.shape[0]):
        out_ref[s] = q


def project_step(parts, start, transfer, copies, step):
    blocks, excite, width = parts.shape
    return pl.pallas_call(
        project_kernel,
        grid=(1,),
        out_shape=(
            jax.ShapeDtypeStruct((excite, width), BF16),
            jax.ShapeDtypeStruct((copies, excite, width), BF16),
        ),
        in_specs=[
            pl.BlockSpec(parts.shape, lambda i: (0, 0, 0)),
            pl.BlockSpec((1, excite, width), lambda i: (step, 0, 0)),
            pl.BlockSpec(transfer.shape, lambda i: (0, 0)),
        ],
        out_specs=(
            pl.BlockSpec((excite, width), lambda i: (0, 0)),
            pl.BlockSpec((copies, excite, width), lambda i: (0, 0, 0)),
        ),
        compiler_params=params(8),
        name="project_step",
    )(parts, start, transfer)


def summed(parts_ref):
    total = parts_ref[0].astype(F32)
    for o in range(1, parts_ref.shape[0]):
        total = total + parts_ref[o].astype(F32)
    return total.astype(BF16)


def currents_kernel(incoming_ref, expanded_ref, parts_ref,
                    f0_ref, f1_ref, f2_ref, f3_ref, out_ref, made_ref, sems):
    fields = [f0_ref[...], f1_ref[...], f2_ref[...], f3_ref[...], summed(parts_ref)]
    clusters, pieces, steps, excite, tile = made_ref.shape
    rank = expanded_ref.shape[1]
    copies = []
    for c in range(clusters):
        left = jnp.concatenate([f[:, c * rank:(c + 1) * rank] for f in fields], axis=0)
        for n in range(pieces):
            lanes = slice(n * tile, (n + 1) * tile)
            far = jnp.dot(left, expanded_ref[c, :, lanes], preferred_element_type=F32)
            for t in range(steps):
                made_ref[c, n, t] = (
                    incoming_ref[t, c, :, lanes].astype(F32) - far[t * excite:(t + 1) * excite]).astype(BF16)
            copy = pltpu.make_async_copy(
                made_ref.at[c, n], out_ref.at[:, c, :, pl.ds(n * tile, tile)], sems.at[c, n])
            copy.start()
            copies.append(copy)
    for copy in copies:
        copy.wait()


def final_currents(incoming, expanded, parts, fields, tile=512):
    steps, clusters, excite, unknowns = incoming.shape
    return pl.pallas_call(
        currents_kernel,
        out_shape=jax.ShapeDtypeStruct((steps, clusters, excite, unknowns), BF16),
        in_specs=[VMEM_SPEC] * (3 + len(fields)),
        out_specs=ANY_SPEC,
        scratch_shapes=[
            pltpu.VMEM((clusters, unknowns // tile, steps, excite, tile), BF16),
            pltpu.SemaphoreType.DMA((clusters, unknowns // tile)),
        ],
        compiler_params=params(12),
        name="final_currents",
    )(incoming, expanded, parts, *fields)


def per_device(history, incident, proj_basis, expand_basis, near_inverse, couplings, lags):
    clusters, rank, unknowns = proj_basis.shape
    width = clusters * rank
    taps, src_rows, blocks = couplings.shape[:3]
    pairs = lags.transpose(1, 2, 3, 0)[:, 0]
    senders = src_rows // width
    flat = couplings.reshape(taps, src_rows * blocks, width)
    def gather(copies):
        return lax.all_to_all(copies, "src", 0, 0)

    def scatter(chunks):
        return lax.all_to_all(chunks, "obs", 0, 0)

    mine, spread = project_history(history, proj_basis, pairs)
    arrived = swap(mine, 1)
    top = build_matrices(0, TOP, flat, spread, mine)
    mine = ordered(mine, arrived, top[0], 1, "order_x")
    arrived = swap(mine, 4)
    bottom = build_matrices(4 * TOP, 8 - TOP, flat, spread, mine)
    incoming, expanded, start, transfer = prepare_near(incident, expand_basis, near_inverse, proj_basis, bottom[0])
    w1, w2, w3 = [list(halves) for halves in zip(top, bottom)]
    gathered = ordered(mine, arrived, transfer, 4, "order_y")
    fields, past = [], []
    excite = history.shape[2]
    full = (excite, blocks * width)
    ahead = None
    for step in range(STEPS):
        if step == 0:
            chunks, base = couple(step0_kernel, "step0", blocks, (2,) + full, [gathered], [transfer], w1 + w2 + w3)
        elif step == 1:
            chunks = couple(step1_kernel, "step1", blocks, None, past, [base], w1)
        elif step == 2:
            chunks, ahead = couple(step2_kernel, "step2", blocks, full, past, [base], w1 + w2)
        elif step == 3:
            chunks, ahead = couple(step3_kernel, "step3", blocks, full, past, [ahead], w1 + w3)
        else:
            chunks = couple(step4_kernel, "step4", blocks, None, past[2:], [ahead], w1 + w2)
        parts = scatter(chunks)
        if step + 1 < STEPS:
            field, copies = project_step(parts, start, transfer, senders, step)
            fields.append(field)
            past.append(gather(copies))
    return final_currents(incoming, expanded, parts, fields)


def solution(mesh):
    placed = (
        P(None, ("obs", "src"), None, None),
        P(None, ("obs", "src"), None, None),
        P(("obs", "src"), None, None),
        P(("obs", "src"), None, None),
        P(("obs", "src"), None, None),
        P(None, "obs", None, "src", None),
        P("obs", None, "src", None),
    )
    return jax.shard_map(
        per_device,
        mesh=mesh,
        in_specs=placed,
        out_specs=P(None, ("obs", "src"), None, None),
        check_vma=False,
    )
```

time: 135 us -> 132 us (0.978)
  waiting for transfers between devices: 2.34 us -> 0.02 us
  blocking collectives: 95.3 us -> 96.8 us
    ppermute x6, waiting for transfers between devices: 2.34 us -> 0.02 us  [swap(): lax.ppermute(array, 'src', [(i, i ^ k * stride) for i in range(16)])]
    pallas_call x6 -> x7, Pallas kernels: 18.2 us -> 17.3 us  [the longest x2 7.59 us: build_matrices(): pl.pallas_call(functools.partial(build_kernel, first, rank, depth), out_s...]
  transfers between devices with their start and end apart: 6 -> 6, of which waited for: 2 -> 0; matrix products, arithmetic and copies ran while one was open for 1% -> 0% of each run, Pallas kernels for 10% -> 10%
where the time goes in v3:
time: 132 us; the launch traced here: 131 us
  blocking collectives  96.8 us (73%)
  Pallas kernels  25.4 us (19%)
  starting transfers between devices  8.66 us (7%)
    all_to_all x4, blocking collectives, gather(): return lax.all_to_all(copies, 'src', 0, 0)  51.3 us
    all_to_all x5, blocking collectives, scatter(): return lax.all_to_all(chunks, 'obs', 0, 0)  45.5 us
    ppermute x6, starting transfers between devices, swap(): lax.ppermute(array, 'src', [(i, i ^ k * stride) for i in range(16)])  8.66 us
    pallas_call x2, Pallas kernels, build_matrices(): pl.pallas_call(functools.partial(build_kernel, first, rank, depth), out_s...  7.59 us
    pallas_call x5, Pallas kernels, couple(): pl.pallas_call(kernel, out_shape=shapes, in_specs=[VMEM_SPEC] * (len(gath...  7.45 us
    pallas_call x1, Pallas kernels, prepare_near(): pl.pallas_call(functools.partial(near_kernel, tile), out_shape=(jax.Shape...  5.06 us
  transfers between devices with their start and end apart: 6, of which 0 were waited for; matrix products, arithmetic and copies ran while one was open for 0% of the time, Pallas kernels for 10%

profile of v3, /device:TPU:0, one launch (start us, length us, event | category | flops | bytes accessed | tf_op | source)
XLA Modules:
  0.0 131.3 jit_solution(491281483990774145)
XLA Ops:
  0.0 2.5 %project_history.1 = (bf16[3,64,128]{2,1,0:T(8,128)(2,1)S(1)}, f32[32,1024]{1,0:T(8,128)S(1)}) custom-call(bf16[3,2,64,1536]{3,2,1,0:T(8,128)(2,1)} %history_ref.1, bf16[2,64,1536]{2,1,0:T(8,128)(2,1)} %proj_ref.3, s32[8,2,32]{2,1,0:T(2,128)} %bitcast.8), custom_call_target="tpu_custom_call" | custom-call | tf_op jit(solution)/shard_map/project_history/pallas_call | solution.py:70
  2.5 3.2 %collective-permute-start.2 = (bf16[3,64,128]{2,1,0:T(8,128)(2,1)S(1)}, bf16[3,64,128]{2,1,0:T(8,128)(2,1)S(1)}, u32[]{:S(2)}, u32[]{:S(2)}) collective-permute-start(bf16[3,64,128]{2,1,0:T(8,128)(2,1)S(1)} %get-tuple-element.32.after_ref.own_ref), channel_id=1, source_target_pairs={{0,2},{1,3},{2,0},{3,1},{4,6},{5,7},{6,4},{7,5},{8,10},{9,11},{10,... | collective-permute-start | bytes 147464 | tf_op jit(solution)/shard_map/ppermute | solution.py:97
  5.6 1.1 collective-permute-start.1
  6.8 0.0 collective-permute-start
  6.8 0.0 slice-start
  6.8 0.0 slice-start.1
  6.8 4.6 %build_matrices0.1 = (bf16[1280,1024]{1,0:T(8,128)(2,1)S(1)}, bf16[1280,1024]{1,0:T(8,128)(2,1)S(1)}, bf16[1280,1024]{1,0:T(8,128)(2,1)S(1)}) custom-call(bf16[2,16384,128]{2,1,0:T(8,128)(2,1)} %bitcast.9, f32[32,1024]{1,0:T(8,128)S(1)} %get-tuple-element.31.spread_ref, bf16[3,64,128]{2,1,0:T(8,128)(2,1)S(1)} %get-tuple-element.32.after_ref.own_ref), custom_call_target="tpu_custom_call" | custom-call | flops 4026531840 | bytes 13107200 | tf_op jit(solution)/shard_map/build_matrices0/pallas_call | solution.py:222
  11.4 0.0 collective-permute-done.2.by2_ref
  11.4 0.0 collective-permute-done.1.by3_ref
  11.4 0.0 collective-permute-done.by1_ref
  11.4 0.0 slice-start.2
  11.5 0.0 copy-start
  11.5 0.0 copy-start.1
  11.5 0.0 copy-start.2
  11.5 3.3 %collective-permute-start.5 = (bf16[4,3,64,128]{3,2,1,0:T(8,128)(2,1)S(1)}, bf16[4,3,64,128]{3,2,1,0:T(8,128)(2,1)S(1)}, u32[]{:S(2)}, u32[]{:S(2)}) collective-permute-start(bf16[4,3,64,128]{3,2,1,0:T(8,128)(2,1)S(1)} %order_x.1.after_ref.own_ref), channel_id=1, source_target_pairs={{0,8},{1,9},{2,10},{3,11},{4,12},{5,13},{6,14},{7,15},{8,0},{9,1},... | collective-permute-start | bytes 589832 | tf_op jit(solution)/shard_map/ppermute | solution.py:97
  14.8 1.1 collective-permute-start.4
  15.9 0.0 collective-permute-start.3
  15.9 3.0 %build_matrices20.1 = (bf16[768,1024]{1,0:T(8,128)(2,1)S(1)}, bf16[768,1024]{1,0:T(8,128)(2,1)S(1)}, bf16[768,1024]{1,0:T(8,128)(2,1)S(1)}) custom-call(bf16[2,16384,128]{2,1,0:T(8,128)(2,1)} %bitcast.10, f32[32,1024]{1,0:T(8,128)S(1)} %get-tuple-element.31.spread_ref, bf16[4,3,64,128]{3,2,1,0:T(8,128)(2,1)S(1)} %order_x.1.after_ref.own_ref), custom_call_target="tpu_custom_call" | custom-call | flops 2415919104 | bytes 7864320 | tf_op jit(solution)/shard_map/build_matrices20/pallas_call | solution.py:222
  18.9 0.0 slice-done
  18.9 0.0 slice-done.1
  18.9 0.0 slice-done.2
  18.9 0.0 copy-done
  18.9 0.0 copy-done.1
  18.9 0.0 copy-done.2
  18.9 5.1 %prepare_near.1 = (bf16[5,2,64,1536]{3,2,1,0:T(8,128)(2,1)S(1)}, bf16[2,64,1536]{2,1,0:T(8,128)(2,1)S(1)}, f32[5,64,128]{2,1,0:T(8,128)S(1)}, bf16[256,128]{1,0:T(8,128)(2,1)S(1)}) custom-call(bf16[5,2,64,1536]{3,2,1,0:T(8,128)(2,1)S(1)} %copy-done.1, bf16[2,64,1536]{2,1,0:T(8,128)(2,1)S(1)} %copy-done.2, bf16[2,1536,1536]{2,1,0:T(8,128)(2,1)S(1)} %bitcast.7, ...), custom_call_target="tpu_custom_call" | custom-call | flops 3774873600 | bytes 9437184 | tf_op jit(solution)/shard_map/prepare_near/pallas_call | solution.py:146
  24.0 0.0 collective-permute-done.5.by2_ref
  24.0 0.0 collective-permute-done.4.by3_ref
  24.0 0.0 collective-permute-done.3.by1_ref
  24.0 0.1 order_y.1.history_ref
  24.1 2.3 %step0.1 = (bf16[8,64,128]{2,1,0:T(8,128)(2,1)S(1)}, f32[2,64,1024]{2,1,0:T(8,128)S(1)}) custom-call(bf16[4,4,3,64,128]{4,3,2,1,0:T(8,128)(2,1)S(1)} %order_y.1.history_ref, bf16[256,128]{1,0:T(8,128)(2,1)S(1)} %get-tuple-element.37.after_ref.transfer_ref, bf16[1280,1024]{1,0:T(8,128)(2,1)S(1)} %get-tuple-element.33.after_ref.w1a_ref, ...), custom_call_target="tpu_custom_call" | custom-call | tf_op jit(solution)/shard_map/step0/pallas_call | solution.py:300
  26.4 11.2 %all_to_all.45.parts_ref = bf16[8,64,128]{2,1,0:T(8,128)(2,1)S(1)} all-to-all(bf16[8,64,128]{2,1,0:T(8,128)(2,1)S(1)} %get-tuple-element.42), channel_id=1, replica_groups=mesh['obs'=8,'src'=16] {'obs'}, dimensions={0} | all-to-all | bytes 262144 | tf_op jit(solution)/shard_map/all_to_all | solution.py:403
  37.6 0.2 project_step.4
  37.8 16.5 %all_to_all.46.q0_ref = bf16[16,64,128]{2,1,0:T(8,128)(2,1)S(1)} all-to-all(bf16[16,64,128]{2,1,0:T(8,128)(2,1)S(1)} %get-tuple-element.44), channel_id=1, replica_groups=mesh['obs'=8,'src'=16] {'src'}, dimensions={0} | all-to-all | bytes 524288 | tf_op jit(solution)/shard_map/all_to_all | solution.py:400
  54.3 0.8 step1.1
  55.1 8.7 %all_to_all.47.parts_ref = bf16[8,64,128]{2,1,0:T(8,128)(2,1)S(1)} all-to-all(bf16[8,64,128]{2,1,0:T(8,128)(2,1)S(1)} %step1.1), channel_id=1, replica_groups=mesh['obs'=8,'src'=16] {'obs'}, dimensions={0} | all-to-all | bytes 262144 | tf_op jit(solution)/shard_map/all_to_all | solution.py:403
  63.8 0.2 project_step.5
  64.0 11.6 %all_to_all.48.q1_ref = bf16[16,64,128]{2,1,0:T(8,128)(2,1)S(1)} all-to-all(bf16[16,64,128]{2,1,0:T(8,128)(2,1)S(1)} %get-tuple-element.46), channel_id=1, replica_groups=mesh['obs'=8,'src'=16] {'src'}, dimensions={0} | all-to-all | bytes 524288 | tf_op jit(solution)/shard_map/all_to_all | solution.py:400
  75.6 1.4 %step2.1 = (bf16[8,64,128]{2,1,0:T(8,128)(2,1)S(1)}, f32[64,1024]{1,0:T(8,128)S(1)}) custom-call(bf16[16,64,128]{2,1,0:T(8,128)(2,1)S(1)} %all_to_all.46.q0_ref, bf16[16,64,128]{2,1,0:T(8,128)(2,1)S(1)} %all_to_all.48.q1_ref, f32[2,64,1024]{2,1,0:T(8,128)S(1)} %get-tuple-element.45.base_ref, bf16[1280,1024]{1,0:T(8,128)(2,1)S(1)} %get-tuple-element.33.after_ref.w1a_ref, ...), custom_call_target="tpu_custom_call" | custom-call | tf_op jit(solution)/shard_map/step2/pallas_call | solution.py:300
  77.0 8.5 %all_to_all.49.parts_ref = bf16[8,64,128]{2,1,0:T(8,128)(2,1)S(1)} all-to-all(bf16[8,64,128]{2,1,0:T(8,128)(2,1)S(1)} %get-tuple-element.47), channel_id=1, replica_groups=mesh['obs'=8,'src'=16] {'obs'}, dimensions={0} | all-to-all | bytes 262144 | tf_op jit(solution)/shard_map/all_to_all | solution.py:403
  85.5 0.2 project_step.6
  85.7 11.6 %all_to_all.50.q2_ref = bf16[16,64,128]{2,1,0:T(8,128)(2,1)S(1)} all-to-all(bf16[16,64,128]{2,1,0:T(8,128)(2,1)S(1)} %get-tuple-element.48), channel_id=1, replica_groups=mesh['obs'=8,'src'=16] {'src'}, dimensions={0} | all-to-all | bytes 524288 | tf_op jit(solution)/shard_map/all_to_all | solution.py:400
  97.3 1.4 %step3.1 = (bf16[8,64,128]{2,1,0:T(8,128)(2,1)S(1)}, f32[64,1024]{1,0:T(8,128)S(1)}) custom-call(bf16[16,64,128]{2,1,0:T(8,128)(2,1)S(1)} %all_to_all.46.q0_ref, bf16[16,64,128]{2,1,0:T(8,128)(2,1)S(1)} %all_to_all.48.q1_ref, bf16[16,64,128]{2,1,0:T(8,128)(2,1)S(1)} %all_to_all.50.q2_ref, f32[64,1024]{1,0:T(8,128)S(1)} %get-tuple-element.49.base_ref, ...), custom_call_target="tpu_custom_call" | custom-call | tf_op jit(solution)/shard_map/step3/pallas_call | solution.py:300
  98.7 8.5 %all_to_all.51.parts_ref = bf16[8,64,128]{2,1,0:T(8,128)(2,1)S(1)} all-to-all(bf16[8,64,128]{2,1,0:T(8,128)(2,1)S(1)} %get-tuple-element.50), channel_id=1, replica_groups=mesh['obs'=8,'src'=16] {'obs'}, dimensions={0} | all-to-all | bytes 262144 | tf_op jit(solution)/shard_map/all_to_all | solution.py:403
  107.2 0.2 project_step.7
  107.3 11.6 %all_to_all.52.q3_ref = bf16[16,64,128]{2,1,0:T(8,128)(2,1)S(1)} all-to-all(bf16[16,64,128]{2,1,0:T(8,128)(2,1)S(1)} %get-tuple-element.51), channel_id=1, replica_groups=mesh['obs'=8,'src'=16] {'src'}, dimensions={0} | all-to-all | bytes 524288 | tf_op jit(solution)/shard_map/all_to_all | solution.py:400
  118.9 1.6 %step4.1 = bf16[8,64,128]{2,1,0:T(8,128)(2,1)S(1)} custom-call(bf16[16,64,128]{2,1,0:T(8,128)(2,1)S(1)} %all_to_all.50.q2_ref, bf16[16,64,128]{2,1,0:T(8,128)(2,1)S(1)} %all_to_all.52.q3_ref, f32[64,1024]{1,0:T(8,128)S(1)} %get-tuple-element.52.base_ref, bf16[1280,1024]{1,0:T(8,128)(2,1)S(1)} %get-tuple-element.33.after_ref.w1a_ref, ...), custom_call_target="tpu_custom_call" | custom-call | tf_op jit(solution)/shard_map/step4/pallas_call | solution.py:300
  120.5 8.5 %all_to_all.53.parts_ref = bf16[8,64,128]{2,1,0:T(8,128)(2,1)S(1)} all-to-all(bf16[8,64,128]{2,1,0:T(8,128)(2,1)S(1)} %step4.1), channel_id=1, replica_groups=mesh['obs'=8,'src'=16] {'obs'}, dimensions={0} | all-to-all | bytes 262144 | tf_op jit(solution)/shard_map/all_to_all | solution.py:403
  129.0 2.1 %final_currents.1 = bf16[5,2,64,1536]{3,2,1,0:T(8,128)(2,1)} custom-call(bf16[5,2,64,1536]{3,2,1,0:T(8,128)(2,1)S(1)} %get-tuple-element.35.incoming_ref, bf16[2,64,1536]{2,1,0:T(8,128)(2,1)S(1)} %get-tuple-element.36.expanded_ref, bf16[8,64,128]{2,1,0:T(8,128)(2,1)S(1)} %all_to_all.53.parts_ref, bf16[64,128]{1,0:T(8,128)(2,1)S(1)} %get-tuple-element.53.f0_ref, ...), custom_call_target="tpu_custom_call" | custom-call | tf_op jit(solution)/shard_map/final_currents/pallas_call | solution.py:378
  (2 shorter events, 0.0 us)
Async XLA Ops:
  2.5 8.9 %collective-permute-start.2 = (bf16[3,64,128]{2,1,0:T(8,128)(2,1)S(1)}, bf16[3,64,128]{2,1,0:T(8,128)(2,1)S(1)}, u32[]{:S(2)}, u32[]{:S(2)}) collective-permute-start(bf16[3,64,128]{2,1,0:T(8,128)(2,1)S(1)} %get-tuple-element.32.after_ref.own_ref), channel_id=1, source_target_pairs={{0,2},{1,3},{2,0},{3,1},{4,6},{5,7},{6,4},{7,5},{8,10},{9,11},{10,... | collective-permute-start | bytes 147464 | tf_op jit(solution)/shard_map/ppermute | solution.py:97
  5.6 5.8 %collective-permute-start.1 = (bf16[3,64,128]{2,1,0:T(8,128)(2,1)S(1)}, bf16[3,64,128]{2,1,0:T(8,128)(2,1)S(1)}, u32[]{:S(2)}, u32[]{:S(2)}) collective-permute-start(bf16[3,64,128]{2,1,0:T(8,128)(2,1)S(1)} %get-tuple-element.32.after_ref.own_ref), channel_id=1, source_target_pairs={{0,3},{1,2},{2,1},{3,0},{4,7},{5,6},{6,5},{7,4},{8,11},{9,10},{10,... | collective-permute-start | bytes 147464 | tf_op jit(solution)/shard_map/ppermute | solution.py:97
  6.8 4.6 %collective-permute-start = (bf16[3,64,128]{2,1,0:T(8,128)(2,1)S(1)}, bf16[3,64,128]{2,1,0:T(8,128)(2,1)S(1)}, u32[]{:S(2)}, u32[]{:S(2)}) collective-permute-start(bf16[3,64,128]{2,1,0:T(8,128)(2,1)S(1)} %get-tuple-element.32.after_ref.own_ref), channel_id=1, source_target_pairs={{0,1},{1,0},{2,3},{3,2},{4,5},{5,4},{6,7},{7,6},{8,9},{9,8},{10,11... | collective-permute-start | bytes 147464 | tf_op jit(solution)/shard_map/ppermute | solution.py:97
  6.8 12.1 %slice-start = ((s8[9437184]{0:T(1024)(128)(4,1)}), s8[4194304]{0:T(1024)(128)(4,1)S(1)}, s32[]{:S(2)}) async-start(s8[9437184]{0:T(1024)(128)(4,1)} %bitcast.6), calls=%async_computation.9 | async-start | bytes 8388608
  6.8 12.1 %slice-start.1 = ((s8[9437184]{0:T(1024)(128)(4,1)}), s8[4194304]{0:T(1024)(128)(4,1)S(1)}, s32[]{:S(2)}) async-start(s8[9437184]{0:T(1024)(128)(4,1)} %bitcast.6), calls=%async_computation.10 | async-start | bytes 8388608
  11.4 7.4 %slice-start.2 = ((s8[9437184]{0:T(1024)(128)(4,1)}), s8[1048576]{0:T(1024)(128)(4,1)S(1)}, s32[]{:S(2)}) async-start(s8[9437184]{0:T(1024)(128)(4,1)} %bitcast.6), calls=%async_computation.11 | async-start | bytes 2097152
  11.5 7.4 %copy-start = (bf16[2,64,1536]{2,1,0:T(8,128)(2,1)S(1)}, bf16[2,64,1536]{2,1,0:T(8,128)(2,1)}, u32[]{:S(2)}) copy-start(bf16[2,64,1536]{2,1,0:T(8,128)(2,1)} %proj_ref.3) | copy-start | bytes 1179652
  11.5 7.4 %copy-start.1 = (bf16[5,2,64,1536]{3,2,1,0:T(8,128)(2,1)S(1)}, bf16[5,2,64,1536]{3,2,1,0:T(8,128)(2,1)}, u32[]{:S(2)}) copy-start(bf16[5,2,64,1536]{3,2,1,0:T(8,128)(2,1)} %incident_ref.1) | copy-start | bytes 5898244
  11.5 7.4 %copy-start.2 = (bf16[2,64,1536]{2,1,0:T(8,128)(2,1)S(1)}, bf16[2,64,1536]{2,1,0:T(8,128)(2,1)}, u32[]{:S(2)}) copy-start(bf16[2,64,1536]{2,1,0:T(8,128)(2,1)} %expand_ref.1) | copy-start | bytes 1179652
  11.5 12.5 %collective-permute-start.5 = (bf16[4,3,64,128]{3,2,1,0:T(8,128)(2,1)S(1)}, bf16[4,3,64,128]{3,2,1,0:T(8,128)(2,1)S(1)}, u32[]{:S(2)}, u32[]{:S(2)}) collective-permute-start(bf16[4,3,64,128]{3,2,1,0:T(8,128)(2,1)S(1)} %order_x.1.after_ref.own_ref), channel_id=1, source_target_pairs={{0,8},{1,9},{2,10},{3,11},{4,12},{5,13},{6,14},{7,15},{8,0},{9,1},... | collective-permute-start | bytes 589832 | tf_op jit(solution)/shard_map/ppermute | solution.py:97
  14.8 9.2 %collective-permute-start.4 = (bf16[4,3,64,128]{3,2,1,0:T(8,128)(2,1)S(1)}, bf16[4,3,64,128]{3,2,1,0:T(8,128)(2,1)S(1)}, u32[]{:S(2)}, u32[]{:S(2)}) collective-permute-start(bf16[4,3,64,128]{3,2,1,0:T(8,128)(2,1)S(1)} %order_x.1.after_ref.own_ref), channel_id=1, source_target_pairs={{0,12},{1,13},{2,14},{3,15},{4,8},{5,9},{6,10},{7,11},{8,4},{9,5},... | collective-permute-start | bytes 589832 | tf_op jit(solution)/shard_map/ppermute | solution.py:97
  15.9 8.2 %collective-permute-start.3 = (bf16[4,3,64,128]{3,2,1,0:T(8,128)(2,1)S(1)}, bf16[4,3,64,128]{3,2,1,0:T(8,128)(2,1)S(1)}, u32[]{:S(2)}, u32[]{:S(2)}) collective-permute-start(bf16[4,3,64,128]{3,2,1,0:T(8,128)(2,1)S(1)} %order_x.1.after_ref.own_ref), channel_id=1, source_target_pairs={{0,4},{1,5},{2,6},{3,7},{4,0},{5,1},{6,2},{7,3},{8,12},{9,13},{10,... | collective-permute-start | bytes 589832 | tf_op jit(solution)/shard_map/ppermute | solution.py:97

commit v4 on v3

--- a/solution.py
+++ b/solution.py
@@ -351,38 +351,34 @@
     return total.astype(BF16)
 
 
-def currents_kernel(incoming_ref, expanded_ref, parts_ref,
-                    f0_ref, f1_ref, f2_ref, f3_ref, out_ref, made_ref, sems):
+def currents_kernel(incoming_ref, expanded_ref, parts_ref, f0_ref, f1_ref, f2_ref, f3_ref, out_ref, made_ref, sems):
     fields = [f0_ref[...], f1_ref[...], f2_ref[...], f3_ref[...], summed(parts_ref)]
-    clusters, pieces, steps, excite, tile = made_ref.shape
+    steps, clusters, excite, unknowns = made_ref.shape
     rank = expanded_ref.shape[1]
     copies = []
     for c in range(clusters):
-        left = jnp.concatenate([f[:, c * rank:(c + 1) * rank] for f in fields], axis=0)
-        for n in range(pieces):
-            lanes = slice(n * tile, (n + 1) * tile)
-            far = jnp.dot(left, expanded_ref[c, :, lanes], preferred_element_type=F32)
-            for t in range(steps):
-                made_ref[c, n, t] = (
-                    incoming_ref[t, c, :, lanes].astype(F32) - far[t * excite:(t + 1) * excite]).astype(BF16)
-            copy = pltpu.make_async_copy(
-                made_ref.at[c, n], out_ref.at[:, c, :, pl.ds(n * tile, tile)], sems.at[c, n])
-            copy.start()
-            copies.append(copy)
+        for first, last in ((0, steps // 2), (steps // 2, steps)):
+            left = jnp.concatenate([f[:, c * rank:(c + 1) * rank] for f in fields[first:last]], axis=0)
+            far = jnp.dot(left, expanded_ref[c], preferred_element_type=F32)
+            for t in range(first, last):
+                own = far[(t - first) * excite:(t - first + 1) * excite]
+                made_ref[t, c] = (incoming_ref[t, c].astype(F32) - own).astype(BF16)
+                copy = pltpu.make_async_copy(made_ref.at[t, c], out_ref.at[t, c], sems.at[t, c])
+                copy.start()
+                copies.append(copy)
     for copy in copies:
         copy.wait()
 
 
-def final_currents(incoming, expanded, parts, fields, tile=512):
-    steps, clusters, excite, unknowns = incoming.shape
+def final_currents(incoming, expanded, parts, fields):
     return pl.pallas_call(
         currents_kernel,
-        out_shape=jax.ShapeDtypeStruct((steps, clusters, excite, unknowns), BF16),
+        out_shape=jax.ShapeDtypeStruct(incoming.shape, BF16),
         in_specs=[VMEM_SPEC] * (3 + len(fields)),
         out_specs=ANY_SPEC,
         scratch_shapes=[
-            pltpu.VMEM((clusters, unknowns // tile, steps, excite, tile), BF16),
-            pltpu.SemaphoreType.DMA((clusters, unknowns // tile)),
+            pltpu.VMEM(incoming.shape, BF16),
+            pltpu.SemaphoreType.DMA(incoming.shape[:2]),
         ],
         compiler_params=params(12),
         name="final_currents",

time: 132 us -> 132 us (level)
  no operation moved by 1% of the time
where the time goes in v4:
time: 132 us; the launch traced here: 131 us
  blocking collectives  96.8 us (73%)
  Pallas kernels  24.9 us (19%)
  starting transfers between devices  8.66 us (7%)
    all_to_all x4, blocking collectives, gather(): return lax.all_to_all(copies, 'src', 0, 0)  51.3 us
    all_to_all x5, blocking collectives, scatter(): return lax.all_to_all(chunks, 'obs', 0, 0)  45.5 us
    ppermute x6, starting transfers between devices, swap(): lax.ppermute(array, 'src', [(i, i ^ k * stride) for i in range(16)])  8.66 us
    pallas_call x2, Pallas kernels, build_matrices(): pl.pallas_call(functools.partial(build_kernel, first, rank, depth), out_s...  7.59 us
    pallas_call x5, Pallas kernels, couple(): pl.pallas_call(kernel, out_shape=shapes, in_specs=[VMEM_SPEC] * (len(gath...  7.45 us
    pallas_call x1, Pallas kernels, prepare_near(): pl.pallas_call(functools.partial(near_kernel, tile), out_shape=(jax.Shape...  5.06 us
  transfers between devices with their start and end apart: 6, of which 0 were waited for; matrix products, arithmetic and copies ran while one was open for 0% of the time, Pallas kernels for 10%

profile of v4, /device:TPU:0, one launch (start us, length us, event | category | flops | bytes accessed | tf_op | source)
XLA Modules:
  0.0 130.8 jit_solution(8580693801111955383)
XLA Ops:
  0.0 2.5 %project_history.1 = (bf16[3,64,128]{2,1,0:T(8,128)(2,1)S(1)}, f32[32,1024]{1,0:T(8,128)S(1)}) custom-call(bf16[3,2,64,1536]{3,2,1,0:T(8,128)(2,1)} %history_ref.1, bf16[2,64,1536]{2,1,0:T(8,128)(2,1)} %proj_ref.3, s32[8,2,32]{2,1,0:T(2,128)} %bitcast.8), custom_call_target="tpu_custom_call" | custom-call | tf_op jit(solution)/shard_map/project_history/pallas_call | solution.py:70
  2.5 3.2 %collective-permute-start.2 = (bf16[3,64,128]{2,1,0:T(8,128)(2,1)S(1)}, bf16[3,64,128]{2,1,0:T(8,128)(2,1)S(1)}, u32[]{:S(2)}, u32[]{:S(2)}) collective-permute-start(bf16[3,64,128]{2,1,0:T(8,128)(2,1)S(1)} %get-tuple-element.32.after_ref.own_ref), channel_id=1, source_target_pairs={{0,2},{1,3},{2,0},{3,1},{4,6},{5,7},{6,4},{7,5},{8,10},{9,11},{10,... | collective-permute-start | bytes 147464 | tf_op jit(solution)/shard_map/ppermute | solution.py:97
  5.6 1.1 collective-permute-start.1
  6.8 0.0 collective-permute-start
  6.8 0.0 slice-start
  6.8 0.0 slice-start.1
  6.8 4.6 %build_matrices0.1 = (bf16[1280,1024]{1,0:T(8,128)(2,1)S(1)}, bf16[1280,1024]{1,0:T(8,128)(2,1)S(1)}, bf16[1280,1024]{1,0:T(8,128)(2,1)S(1)}) custom-call(bf16[2,16384,128]{2,1,0:T(8,128)(2,1)} %bitcast.9, f32[32,1024]{1,0:T(8,128)S(1)} %get-tuple-element.31.spread_ref, bf16[3,64,128]{2,1,0:T(8,128)(2,1)S(1)} %get-tuple-element.32.after_ref.own_ref), custom_call_target="tpu_custom_call" | custom-call | flops 4026531840 | bytes 13107200 | tf_op jit(solution)/shard_map/build_matrices0/pallas_call | solution.py:222
  11.4 0.0 collective-permute-done.2.by2_ref
  11.4 0.0 collective-permute-done.1.by3_ref
  11.4 0.0 collective-permute-done.by1_ref
  11.4 0.0 slice-start.2
  11.5 0.0 copy-start
  11.5 0.0 copy-start.1
  11.5 0.0 copy-start.2
  11.5 3.3 %collective-permute-start.5 = (bf16[4,3,64,128]{3,2,1,0:T(8,128)(2,1)S(1)}, bf16[4,3,64,128]{3,2,1,0:T(8,128)(2,1)S(1)}, u32[]{:S(2)}, u32[]{:S(2)}) collective-permute-start(bf16[4,3,64,128]{3,2,1,0:T(8,128)(2,1)S(1)} %order_x.1.after_ref.own_ref), channel_id=1, source_target_pairs={{0,8},{1,9},{2,10},{3,11},{4,12},{5,13},{6,14},{7,15},{8,0},{9,1},... | collective-permute-start | bytes 589832 | tf_op jit(solution)/shard_map/ppermute | solution.py:97
  14.8 1.1 collective-permute-start.4
  15.9 0.0 collective-permute-start.3
  15.9 3.0 %build_matrices20.1 = (bf16[768,1024]{1,0:T(8,128)(2,1)S(1)}, bf16[768,1024]{1,0:T(8,128)(2,1)S(1)}, bf16[768,1024]{1,0:T(8,128)(2,1)S(1)}) custom-call(bf16[2,16384,128]{2,1,0:T(8,128)(2,1)} %bitcast.10, f32[32,1024]{1,0:T(8,128)S(1)} %get-tuple-element.31.spread_ref, bf16[4,3,64,128]{3,2,1,0:T(8,128)(2,1)S(1)} %order_x.1.after_ref.own_ref), custom_call_target="tpu_custom_call" | custom-call | flops 2415919104 | bytes 7864320 | tf_op jit(solution)/shard_map/build_matrices20/pallas_call | solution.py:222
  18.9 0.0 slice-done
  18.9 0.0 slice-done.1
  18.9 0.0 slice-done.2
  18.9 0.0 copy-done
  18.9 0.0 copy-done.1
  18.9 0.0 copy-done.2
  18.9 5.1 %prepare_near.1 = (bf16[5,2,64,1536]{3,2,1,0:T(8,128)(2,1)S(1)}, bf16[2,64,1536]{2,1,0:T(8,128)(2,1)S(1)}, f32[5,64,128]{2,1,0:T(8,128)S(1)}, bf16[256,128]{1,0:T(8,128)(2,1)S(1)}) custom-call(bf16[5,2,64,1536]{3,2,1,0:T(8,128)(2,1)S(1)} %copy-done.1, bf16[2,64,1536]{2,1,0:T(8,128)(2,1)S(1)} %copy-done.2, bf16[2,1536,1536]{2,1,0:T(8,128)(2,1)S(1)} %bitcast.7, ...), custom_call_target="tpu_custom_call" | custom-call | flops 3774873600 | bytes 9437184 | tf_op jit(solution)/shard_map/prepare_near/pallas_call | solution.py:146
  24.0 0.0 collective-permute-done.5.by2_ref
  24.0 0.0 collective-permute-done.4.by3_ref
  24.0 0.0 collective-permute-done.3.by1_ref
  24.0 0.1 order_y.1.history_ref
  24.1 2.3 %step0.1 = (bf16[8,64,128]{2,1,0:T(8,128)(2,1)S(1)}, f32[2,64,1024]{2,1,0:T(8,128)S(1)}) custom-call(bf16[4,4,3,64,128]{4,3,2,1,0:T(8,128)(2,1)S(1)} %order_y.1.history_ref, bf16[256,128]{1,0:T(8,128)(2,1)S(1)} %get-tuple-element.37.after_ref.transfer_ref, bf16[1280,1024]{1,0:T(8,128)(2,1)S(1)} %get-tuple-element.33.after_ref.w1a_ref, ...), custom_call_target="tpu_custom_call" | custom-call | tf_op jit(solution)/shard_map/step0/pallas_call | solution.py:300
  26.4 11.2 %all_to_all.45.parts_ref = bf16[8,64,128]{2,1,0:T(8,128)(2,1)S(1)} all-to-all(bf16[8,64,128]{2,1,0:T(8,128)(2,1)S(1)} %get-tuple-element.42), channel_id=1, replica_groups=mesh['obs'=8,'src'=16] {'obs'}, dimensions={0} | all-to-all | bytes 262144 | tf_op jit(solution)/shard_map/all_to_all | solution.py:399
  37.6 0.2 project_step.4
  37.8 16.5 %all_to_all.46.q0_ref = bf16[16,64,128]{2,1,0:T(8,128)(2,1)S(1)} all-to-all(bf16[16,64,128]{2,1,0:T(8,128)(2,1)S(1)} %get-tuple-element.44), channel_id=1, replica_groups=mesh['obs'=8,'src'=16] {'src'}, dimensions={0} | all-to-all | bytes 524288 | tf_op jit(solution)/shard_map/all_to_all | solution.py:396
  54.3 0.8 step1.1
  55.1 8.7 %all_to_all.47.parts_ref = bf16[8,64,128]{2,1,0:T(8,128)(2,1)S(1)} all-to-all(bf16[8,64,128]{2,1,0:T(8,128)(2,1)S(1)} %step1.1), channel_id=1, replica_groups=mesh['obs'=8,'src'=16] {'obs'}, dimensions={0} | all-to-all | bytes 262144 | tf_op jit(solution)/shard_map/all_to_all | solution.py:399
  63.8 0.2 project_step.5
  64.0 11.6 %all_to_all.48.q1_ref = bf16[16,64,128]{2,1,0:T(8,128)(2,1)S(1)} all-to-all(bf16[16,64,128]{2,1,0:T(8,128)(2,1)S(1)} %get-tuple-element.46), channel_id=1, replica_groups=mesh['obs'=8,'src'=16] {'src'}, dimensions={0} | all-to-all | bytes 524288 | tf_op jit(solution)/shard_map/all_to_all | solution.py:396
  75.6 1.4 %step2.1 = (bf16[8,64,128]{2,1,0:T(8,128)(2,1)S(1)}, f32[64,1024]{1,0:T(8,128)S(1)}) custom-call(bf16[16,64,128]{2,1,0:T(8,128)(2,1)S(1)} %all_to_all.46.q0_ref, bf16[16,64,128]{2,1,0:T(8,128)(2,1)S(1)} %all_to_all.48.q1_ref, f32[2,64,1024]{2,1,0:T(8,128)S(1)} %get-tuple-element.45.base_ref, bf16[1280,1024]{1,0:T(8,128)(2,1)S(1)} %get-tuple-element.33.after_ref.w1a_ref, ...), custom_call_target="tpu_custom_call" | custom-call | tf_op jit(solution)/shard_map/step2/pallas_call | solution.py:300
  77.0 8.5 %all_to_all.49.parts_ref = bf16[8,64,128]{2,1,0:T(8,128)(2,1)S(1)} all-to-all(bf16[8,64,128]{2,1,0:T(8,128)(2,1)S(1)} %get-tuple-element.47), channel_id=1, replica_groups=mesh['obs'=8,'src'=16] {'obs'}, dimensions={0} | all-to-all | bytes 262144 | tf_op jit(solution)/shard_map/all_to_all | solution.py:399
  85.5 0.2 project_step.6
  85.7 11.6 %all_to_all.50.q2_ref = bf16[16,64,128]{2,1,0:T(8,128)(2,1)S(1)} all-to-all(bf16[16,64,128]{2,1,0:T(8,128)(2,1)S(1)} %get-tuple-element.48), channel_id=1, replica_groups=mesh['obs'=8,'src'=16] {'src'}, dimensions={0} | all-to-all | bytes 524288 | tf_op jit(solution)/shard_map/all_to_all | solution.py:396
  97.3 1.4 %step3.1 = (bf16[8,64,128]{2,1,0:T(8,128)(2,1)S(1)}, f32[64,1024]{1,0:T(8,128)S(1)}) custom-call(bf16[16,64,128]{2,1,0:T(8,128)(2,1)S(1)} %all_to_all.46.q0_ref, bf16[16,64,128]{2,1,0:T(8,128)(2,1)S(1)} %all_to_all.48.q1_ref, bf16[16,64,128]{2,1,0:T(8,128)(2,1)S(1)} %all_to_all.50.q2_ref, f32[64,1024]{1,0:T(8,128)S(1)} %get-tuple-element.49.base_ref, ...), custom_call_target="tpu_custom_call" | custom-call | tf_op jit(solution)/shard_map/step3/pallas_call | solution.py:300
  98.7 8.5 %all_to_all.51.parts_ref = bf16[8,64,128]{2,1,0:T(8,128)(2,1)S(1)} all-to-all(bf16[8,64,128]{2,1,0:T(8,128)(2,1)S(1)} %get-tuple-element.50), channel_id=1, replica_groups=mesh['obs'=8,'src'=16] {'obs'}, dimensions={0} | all-to-all | bytes 262144 | tf_op jit(solution)/shard_map/all_to_all | solution.py:399
  107.2 0.2 project_step.7
  107.3 11.6 %all_to_all.52.q3_ref = bf16[16,64,128]{2,1,0:T(8,128)(2,1)S(1)} all-to-all(bf16[16,64,128]{2,1,0:T(8,128)(2,1)S(1)} %get-tuple-element.51), channel_id=1, replica_groups=mesh['obs'=8,'src'=16] {'src'}, dimensions={0} | all-to-all | bytes 524288 | tf_op jit(solution)/shard_map/all_to_all | solution.py:396
  118.9 1.6 %step4.1 = bf16[8,64,128]{2,1,0:T(8,128)(2,1)S(1)} custom-call(bf16[16,64,128]{2,1,0:T(8,128)(2,1)S(1)} %all_to_all.50.q2_ref, bf16[16,64,128]{2,1,0:T(8,128)(2,1)S(1)} %all_to_all.52.q3_ref, f32[64,1024]{1,0:T(8,128)S(1)} %get-tuple-element.52.base_ref, bf16[1280,1024]{1,0:T(8,128)(2,1)S(1)} %get-tuple-element.33.after_ref.w1a_ref, ...), custom_call_target="tpu_custom_call" | custom-call | tf_op jit(solution)/shard_map/step4/pallas_call | solution.py:300
  120.5 8.5 %all_to_all.53.parts_ref = bf16[8,64,128]{2,1,0:T(8,128)(2,1)S(1)} all-to-all(bf16[8,64,128]{2,1,0:T(8,128)(2,1)S(1)} %step4.1), channel_id=1, replica_groups=mesh['obs'=8,'src'=16] {'obs'}, dimensions={0} | all-to-all | bytes 262144 | tf_op jit(solution)/shard_map/all_to_all | solution.py:399
  129.0 1.6 %final_currents.1 = bf16[5,2,64,1536]{3,2,1,0:T(8,128)(2,1)} custom-call(bf16[5,2,64,1536]{3,2,1,0:T(8,128)(2,1)S(1)} %get-tuple-element.35.incoming_ref, bf16[2,64,1536]{2,1,0:T(8,128)(2,1)S(1)} %get-tuple-element.36.expanded_ref, bf16[8,64,128]{2,1,0:T(8,128)(2,1)S(1)} %all_to_all.53.parts_ref, bf16[64,128]{1,0:T(8,128)(2,1)S(1)} %get-tuple-element.53.f0_ref, ...), custom_call_target="tpu_custom_call" | custom-call | tf_op jit(solution)/shard_map/final_currents/pallas_call | solution.py:374
  (2 shorter events, 0.0 us)
Async XLA Ops:
  2.5 8.9 %collective-permute-start.2 = (bf16[3,64,128]{2,1,0:T(8,128)(2,1)S(1)}, bf16[3,64,128]{2,1,0:T(8,128)(2,1)S(1)}, u32[]{:S(2)}, u32[]{:S(2)}) collective-permute-start(bf16[3,64,128]{2,1,0:T(8,128)(2,1)S(1)} %get-tuple-element.32.after_ref.own_ref), channel_id=1, source_target_pairs={{0,2},{1,3},{2,0},{3,1},{4,6},{5,7},{6,4},{7,5},{8,10},{9,11},{10,... | collective-permute-start | bytes 147464 | tf_op jit(solution)/shard_map/ppermute | solution.py:97
  5.6 5.8 %collective-permute-start.1 = (bf16[3,64,128]{2,1,0:T(8,128)(2,1)S(1)}, bf16[3,64,128]{2,1,0:T(8,128)(2,1)S(1)}, u32[]{:S(2)}, u32[]{:S(2)}) collective-permute-start(bf16[3,64,128]{2,1,0:T(8,128)(2,1)S(1)} %get-tuple-element.32.after_ref.own_ref), channel_id=1, source_target_pairs={{0,3},{1,2},{2,1},{3,0},{4,7},{5,6},{6,5},{7,4},{8,11},{9,10},{10,... | collective-permute-start | bytes 147464 | tf_op jit(solution)/shard_map/ppermute | solution.py:97
  6.8 4.6 %collective-permute-start = (bf16[3,64,128]{2,1,0:T(8,128)(2,1)S(1)}, bf16[3,64,128]{2,1,0:T(8,128)(2,1)S(1)}, u32[]{:S(2)}, u32[]{:S(2)}) collective-permute-start(bf16[3,64,128]{2,1,0:T(8,128)(2,1)S(1)} %get-tuple-element.32.after_ref.own_ref), channel_id=1, source_target_pairs={{0,1},{1,0},{2,3},{3,2},{4,5},{5,4},{6,7},{7,6},{8,9},{9,8},{10,11... | collective-permute-start | bytes 147464 | tf_op jit(solution)/shard_map/ppermute | solution.py:97
  6.8 12.1 %slice-start = ((s8[9437184]{0:T(1024)(128)(4,1)}), s8[4194304]{0:T(1024)(128)(4,1)S(1)}, s32[]{:S(2)}) async-start(s8[9437184]{0:T(1024)(128)(4,1)} %bitcast.6), calls=%async_computation.9 | async-start | bytes 8388608
  6.8 12.1 %slice-start.1 = ((s8[9437184]{0:T(1024)(128)(4,1)}), s8[4194304]{0:T(1024)(128)(4,1)S(1)}, s32[]{:S(2)}) async-start(s8[9437184]{0:T(1024)(128)(4,1)} %bitcast.6), calls=%async_computation.10 | async-start | bytes 8388608
  11.4 7.4 %slice-start.2 = ((s8[9437184]{0:T(1024)(128)(4,1)}), s8[1048576]{0:T(1024)(128)(4,1)S(1)}, s32[]{:S(2)}) async-start(s8[9437184]{0:T(1024)(128)(4,1)} %bitcast.6), calls=%async_computation.11 | async-start | bytes 2097152
  11.5 7.4 %copy-start = (bf16[2,64,1536]{2,1,0:T(8,128)(2,1)S(1)}, bf16[2,64,1536]{2,1,0:T(8,128)(2,1)}, u32[]{:S(2)}) copy-start(bf16[2,64,1536]{2,1,0:T(8,128)(2,1)} %proj_ref.3) | copy-start | bytes 1179652
  11.5 7.4 %copy-start.1 = (bf16[5,2,64,1536]{3,2,1,0:T(8,128)(2,1)S(1)}, bf16[5,2,64,1536]{3,2,1,0:T(8,128)(2,1)}, u32[]{:S(2)}) copy-start(bf16[5,2,64,1536]{3,2,1,0:T(8,128)(2,1)} %incident_ref.1) | copy-start | bytes 5898244
  11.5 7.4 %copy-start.2 = (bf16[2,64,1536]{2,1,0:T(8,128)(2,1)S(1)}, bf16[2,64,1536]{2,1,0:T(8,128)(2,1)}, u32[]{:S(2)}) copy-start(bf16[2,64,1536]{2,1,0:T(8,128)(2,1)} %expand_ref.1) | copy-start | bytes 1179652
  11.5 12.5 %collective-permute-start.5 = (bf16[4,3,64,128]{3,2,1,0:T(8,128)(2,1)S(1)}, bf16[4,3,64,128]{3,2,1,0:T(8,128)(2,1)S(1)}, u32[]{:S(2)}, u32[]{:S(2)}) collective-permute-start(bf16[4,3,64,128]{3,2,1,0:T(8,128)(2,1)S(1)} %order_x.1.after_ref.own_ref), channel_id=1, source_target_pairs={{0,8},{1,9},{2,10},{3,11},{4,12},{5,13},{6,14},{7,15},{8,0},{9,1},... | collective-permute-start | bytes 589832 | tf_op jit(solution)/shard_map/ppermute | solution.py:97
  14.8 9.2 %collective-permute-start.4 = (bf16[4,3,64,128]{3,2,1,0:T(8,128)(2,1)S(1)}, bf16[4,3,64,128]{3,2,1,0:T(8,128)(2,1)S(1)}, u32[]{:S(2)}, u32[]{:S(2)}) collective-permute-start(bf16[4,3,64,128]{3,2,1,0:T(8,128)(2,1)S(1)} %order_x.1.after_ref.own_ref), channel_id=1, source_target_pairs={{0,12},{1,13},{2,14},{3,15},{4,8},{5,9},{6,10},{7,11},{8,4},{9,5},... | collective-permute-start | bytes 589832 | tf_op jit(solution)/shard_map/ppermute | solution.py:97
  15.9 8.2 %collective-permute-start.3 = (bf16[4,3,64,128]{3,2,1,0:T(8,128)(2,1)S(1)}, bf16[4,3,64,128]{3,2,1,0:T(8,128)(2,1)S(1)}, u32[]{:S(2)}, u32[]{:S(2)}) collective-permute-start(bf16[4,3,64,128]{3,2,1,0:T(8,128)(2,1)S(1)} %order_x.1.after_ref.own_ref), channel_id=1, source_target_pairs={{0,4},{1,5},{2,6},{3,7},{4,0},{5,1},{6,2},{7,3},{8,12},{9,13},{10,... | collective-permute-start | bytes 589832 | tf_op jit(solution)/shard_map/ppermute | solution.py:97

commit v5 on v4

--- a/solution.py
+++ b/solution.py
@@ -213,7 +213,7 @@
                     w3_ref[out, lanes] = k1 * m2
 
 
-def build_matrices(first, pieces, couplings, spread, after, depth=3, clusters_here=4):
+def build_matrices(first, pieces, couplings, spread, after, depth=5, clusters_here=4):
     sources, columns = spread.shape
     taps, count, width = couplings.shape
     blocks = columns // width

time: 132 us -> 131 us (level)
  transfers between devices with their start and end apart: 6 -> 6, of which waited for: 0 -> 0; matrix products, arithmetic and copies ran while one was open for 0% -> 0% of each run, Pallas kernels for 10% -> 9%
where the time goes in v5:
time: 131 us; the launch traced here: 130 us
  blocking collectives  96.8 us (74%)
  Pallas kernels  24.6 us (19%)
  starting transfers between devices  8.66 us (7%)
    all_to_all x4, blocking collectives, gather(): return lax.all_to_all(copies, 'src', 0, 0)  51.3 us
    all_to_all x5, blocking collectives, scatter(): return lax.all_to_all(chunks, 'obs', 0, 0)  45.5 us
    ppermute x6, starting transfers between devices, swap(): lax.ppermute(array, 'src', [(i, i ^ k * stride) for i in range(16)])  8.66 us
    pallas_call x5, Pallas kernels, couple(): pl.pallas_call(kernel, out_shape=shapes, in_specs=[VMEM_SPEC] * (len(gath...  7.46 us
    pallas_call x2, Pallas kernels, build_matrices(): pl.pallas_call(functools.partial(build_kernel, first, rank, depth), out_s...  7.32 us
    pallas_call x1, Pallas kernels, prepare_near(): pl.pallas_call(functools.partial(near_kernel, tile), out_shape=(jax.Shape...  5.06 us
  transfers between devices with their start and end apart: 6, of which 0 were waited for; matrix products, arithmetic and copies ran while one was open for 0% of the time, Pallas kernels for 9%

profile of v5, /device:TPU:0, one launch (start us, length us, event | category | flops | bytes accessed | tf_op | source)
XLA Modules:
  0.0 130.5 jit_solution(4093792684555957918)
XLA Ops:
  0.0 2.5 %project_history.1 = (bf16[3,64,128]{2,1,0:T(8,128)(2,1)S(1)}, f32[32,1024]{1,0:T(8,128)S(1)}) custom-call(bf16[3,2,64,1536]{3,2,1,0:T(8,128)(2,1)} %history_ref.1, bf16[2,64,1536]{2,1,0:T(8,128)(2,1)} %proj_ref.3, s32[8,2,32]{2,1,0:T(2,128)} %bitcast.8), custom_call_target="tpu_custom_call" | custom-call | tf_op jit(solution)/shard_map/project_history/pallas_call | solution.py:70
  2.5 3.2 %collective-permute-start.2 = (bf16[3,64,128]{2,1,0:T(8,128)(2,1)S(1)}, bf16[3,64,128]{2,1,0:T(8,128)(2,1)S(1)}, u32[]{:S(2)}, u32[]{:S(2)}) collective-permute-start(bf16[3,64,128]{2,1,0:T(8,128)(2,1)S(1)} %get-tuple-element.32.after_ref.own_ref), channel_id=1, source_target_pairs={{0,2},{1,3},{2,0},{3,1},{4,6},{5,7},{6,4},{7,5},{8,10},{9,11},{10,... | collective-permute-start | bytes 147464 | tf_op jit(solution)/shard_map/ppermute | solution.py:97
  5.6 1.1 collective-permute-start.1
  6.8 0.0 collective-permute-start
  6.8 0.0 slice-start
  6.8 0.0 slice-start.1
  6.8 4.3 %build_matrices0.1 = (bf16[1280,1024]{1,0:T(8,128)(2,1)S(1)}, bf16[1280,1024]{1,0:T(8,128)(2,1)S(1)}, bf16[1280,1024]{1,0:T(8,128)(2,1)S(1)}) custom-call(bf16[2,16384,128]{2,1,0:T(8,128)(2,1)} %bitcast.9, f32[32,1024]{1,0:T(8,128)S(1)} %get-tuple-element.31.spread_ref, bf16[3,64,128]{2,1,0:T(8,128)(2,1)S(1)} %get-tuple-element.32.after_ref.own_ref), custom_call_target="tpu_custom_call" | custom-call | flops 4026531840 | bytes 13107200 | tf_op jit(solution)/shard_map/build_matrices0/pallas_call | solution.py:222
  11.1 0.0 collective-permute-done.2.by2_ref
  11.1 0.0 collective-permute-done.1.by3_ref
  11.2 0.0 collective-permute-done.by1_ref
  11.2 0.0 slice-start.2
  11.2 0.0 copy-start
  11.2 0.0 copy-start.1
  11.2 0.0 copy-start.2
  11.3 3.3 %collective-permute-start.5 = (bf16[4,3,64,128]{3,2,1,0:T(8,128)(2,1)S(1)}, bf16[4,3,64,128]{3,2,1,0:T(8,128)(2,1)S(1)}, u32[]{:S(2)}, u32[]{:S(2)}) collective-permute-start(bf16[4,3,64,128]{3,2,1,0:T(8,128)(2,1)S(1)} %order_x.1.after_ref.own_ref), channel_id=1, source_target_pairs={{0,8},{1,9},{2,10},{3,11},{4,12},{5,13},{6,14},{7,15},{8,0},{9,1},... | collective-permute-start | bytes 589832 | tf_op jit(solution)/shard_map/ppermute | solution.py:97
  14.5 1.1 collective-permute-start.4
  15.6 0.0 collective-permute-start.3
  15.6 3.0 %build_matrices20.1 = (bf16[768,1024]{1,0:T(8,128)(2,1)S(1)}, bf16[768,1024]{1,0:T(8,128)(2,1)S(1)}, bf16[768,1024]{1,0:T(8,128)(2,1)S(1)}) custom-call(bf16[2,16384,128]{2,1,0:T(8,128)(2,1)} %bitcast.10, f32[32,1024]{1,0:T(8,128)S(1)} %get-tuple-element.31.spread_ref, bf16[4,3,64,128]{3,2,1,0:T(8,128)(2,1)S(1)} %order_x.1.after_ref.own_ref), custom_call_target="tpu_custom_call" | custom-call | flops 2415919104 | bytes 7864320 | tf_op jit(solution)/shard_map/build_matrices20/pallas_call | solution.py:222
  18.6 0.0 slice-done
  18.6 0.0 slice-done.1
  18.6 0.0 slice-done.2
  18.6 0.0 copy-done
  18.6 0.0 copy-done.1
  18.6 0.0 copy-done.2
  18.6 5.1 %prepare_near.1 = (bf16[5,2,64,1536]{3,2,1,0:T(8,128)(2,1)S(1)}, bf16[2,64,1536]{2,1,0:T(8,128)(2,1)S(1)}, f32[5,64,128]{2,1,0:T(8,128)S(1)}, bf16[256,128]{1,0:T(8,128)(2,1)S(1)}) custom-call(bf16[5,2,64,1536]{3,2,1,0:T(8,128)(2,1)S(1)} %copy-done.1, bf16[2,64,1536]{2,1,0:T(8,128)(2,1)S(1)} %copy-done.2, bf16[2,1536,1536]{2,1,0:T(8,128)(2,1)S(1)} %bitcast.7, ...), custom_call_target="tpu_custom_call" | custom-call | flops 3774873600 | bytes 9437184 | tf_op jit(solution)/shard_map/prepare_near/pallas_call | solution.py:146
  23.7 0.0 collective-permute-done.5.by2_ref
  23.7 0.0 collective-permute-done.4.by3_ref
  23.7 0.0 collective-permute-done.3.by1_ref
  23.7 0.1 order_y.1.history_ref
  23.8 2.3 %step0.1 = (bf16[8,64,128]{2,1,0:T(8,128)(2,1)S(1)}, f32[2,64,1024]{2,1,0:T(8,128)S(1)}) custom-call(bf16[4,4,3,64,128]{4,3,2,1,0:T(8,128)(2,1)S(1)} %order_y.1.history_ref, bf16[256,128]{1,0:T(8,128)(2,1)S(1)} %get-tuple-element.37.after_ref.transfer_ref, bf16[1280,1024]{1,0:T(8,128)(2,1)S(1)} %get-tuple-element.33.after_ref.w1a_ref, ...), custom_call_target="tpu_custom_call" | custom-call | tf_op jit(solution)/shard_map/step0/pallas_call | solution.py:300
  26.1 11.2 %all_to_all.45.parts_ref = bf16[8,64,128]{2,1,0:T(8,128)(2,1)S(1)} all-to-all(bf16[8,64,128]{2,1,0:T(8,128)(2,1)S(1)} %get-tuple-element.42), channel_id=1, replica_groups=mesh['obs'=8,'src'=16] {'obs'}, dimensions={0} | all-to-all | bytes 262144 | tf_op jit(solution)/shard_map/all_to_all | solution.py:399
  37.3 0.2 project_step.4
  37.5 16.5 %all_to_all.46.q0_ref = bf16[16,64,128]{2,1,0:T(8,128)(2,1)S(1)} all-to-all(bf16[16,64,128]{2,1,0:T(8,128)(2,1)S(1)} %get-tuple-element.44), channel_id=1, replica_groups=mesh['obs'=8,'src'=16] {'src'}, dimensions={0} | all-to-all | bytes 524288 | tf_op jit(solution)/shard_map/all_to_all | solution.py:396
  54.0 0.8 step1.1
  54.8 8.7 %all_to_all.47.parts_ref = bf16[8,64,128]{2,1,0:T(8,128)(2,1)S(1)} all-to-all(bf16[8,64,128]{2,1,0:T(8,128)(2,1)S(1)} %step1.1), channel_id=1, replica_groups=mesh['obs'=8,'src'=16] {'obs'}, dimensions={0} | all-to-all | bytes 262144 | tf_op jit(solution)/shard_map/all_to_all | solution.py:399
  63.5 0.2 project_step.5
  63.7 11.6 %all_to_all.48.q1_ref = bf16[16,64,128]{2,1,0:T(8,128)(2,1)S(1)} all-to-all(bf16[16,64,128]{2,1,0:T(8,128)(2,1)S(1)} %get-tuple-element.46), channel_id=1, replica_groups=mesh['obs'=8,'src'=16] {'src'}, dimensions={0} | all-to-all | bytes 524288 | tf_op jit(solution)/shard_map/all_to_all | solution.py:396
  75.3 1.4 %step2.1 = (bf16[8,64,128]{2,1,0:T(8,128)(2,1)S(1)}, f32[64,1024]{1,0:T(8,128)S(1)}) custom-call(bf16[16,64,128]{2,1,0:T(8,128)(2,1)S(1)} %all_to_all.46.q0_ref, bf16[16,64,128]{2,1,0:T(8,128)(2,1)S(1)} %all_to_all.48.q1_ref, f32[2,64,1024]{2,1,0:T(8,128)S(1)} %get-tuple-element.45.base_ref, bf16[1280,1024]{1,0:T(8,128)(2,1)S(1)} %get-tuple-element.33.after_ref.w1a_ref, ...), custom_call_target="tpu_custom_call" | custom-call | tf_op jit(solution)/shard_map/step2/pallas_call | solution.py:300
  76.7 8.5 %all_to_all.49.parts_ref = bf16[8,64,128]{2,1,0:T(8,128)(2,1)S(1)} all-to-all(bf16[8,64,128]{2,1,0:T(8,128)(2,1)S(1)} %get-tuple-element.47), channel_id=1, replica_groups=mesh['obs'=8,'src'=16] {'obs'}, dimensions={0} | all-to-all | bytes 262144 | tf_op jit(solution)/shard_map/all_to_all | solution.py:399
  85.2 0.2 project_step.6
  85.4 11.6 %all_to_all.50.q2_ref = bf16[16,64,128]{2,1,0:T(8,128)(2,1)S(1)} all-to-all(bf16[16,64,128]{2,1,0:T(8,128)(2,1)S(1)} %get-tuple-element.48), channel_id=1, replica_groups=mesh['obs'=8,'src'=16] {'src'}, dimensions={0} | all-to-all | bytes 524288 | tf_op jit(solution)/shard_map/all_to_all | solution.py:396
  97.0 1.4 %step3.1 = (bf16[8,64,128]{2,1,0:T(8,128)(2,1)S(1)}, f32[64,1024]{1,0:T(8,128)S(1)}) custom-call(bf16[16,64,128]{2,1,0:T(8,128)(2,1)S(1)} %all_to_all.46.q0_ref, bf16[16,64,128]{2,1,0:T(8,128)(2,1)S(1)} %all_to_all.48.q1_ref, bf16[16,64,128]{2,1,0:T(8,128)(2,1)S(1)} %all_to_all.50.q2_ref, f32[64,1024]{1,0:T(8,128)S(1)} %get-tuple-element.49.base_ref, ...), custom_call_target="tpu_custom_call" | custom-call | tf_op jit(solution)/shard_map/step3/pallas_call | solution.py:300
  98.4 8.5 %all_to_all.51.parts_ref = bf16[8,64,128]{2,1,0:T(8,128)(2,1)S(1)} all-to-all(bf16[8,64,128]{2,1,0:T(8,128)(2,1)S(1)} %get-tuple-element.50), channel_id=1, replica_groups=mesh['obs'=8,'src'=16] {'obs'}, dimensions={0} | all-to-all | bytes 262144 | tf_op jit(solution)/shard_map/all_to_all | solution.py:399
  106.9 0.2 project_step.7
  107.1 11.6 %all_to_all.52.q3_ref = bf16[16,64,128]{2,1,0:T(8,128)(2,1)S(1)} all-to-all(bf16[16,64,128]{2,1,0:T(8,128)(2,1)S(1)} %get-tuple-element.51), channel_id=1, replica_groups=mesh['obs'=8,'src'=16] {'src'}, dimensions={0} | all-to-all | bytes 524288 | tf_op jit(solution)/shard_map/all_to_all | solution.py:396
  118.7 1.6 %step4.1 = bf16[8,64,128]{2,1,0:T(8,128)(2,1)S(1)} custom-call(bf16[16,64,128]{2,1,0:T(8,128)(2,1)S(1)} %all_to_all.50.q2_ref, bf16[16,64,128]{2,1,0:T(8,128)(2,1)S(1)} %all_to_all.52.q3_ref, f32[64,1024]{1,0:T(8,128)S(1)} %get-tuple-element.52.base_ref, bf16[1280,1024]{1,0:T(8,128)(2,1)S(1)} %get-tuple-element.33.after_ref.w1a_ref, ...), custom_call_target="tpu_custom_call" | custom-call | tf_op jit(solution)/shard_map/step4/pallas_call | solution.py:300
  120.2 8.5 %all_to_all.53.parts_ref = bf16[8,64,128]{2,1,0:T(8,128)(2,1)S(1)} all-to-all(bf16[8,64,128]{2,1,0:T(8,128)(2,1)S(1)} %step4.1), channel_id=1, replica_groups=mesh['obs'=8,'src'=16] {'obs'}, dimensions={0} | all-to-all | bytes 262144 | tf_op jit(solution)/shard_map/all_to_all | solution.py:399
  128.7 1.6 %final_currents.1 = bf16[5,2,64,1536]{3,2,1,0:T(8,128)(2,1)} custom-call(bf16[5,2,64,1536]{3,2,1,0:T(8,128)(2,1)S(1)} %get-tuple-element.35.incoming_ref, bf16[2,64,1536]{2,1,0:T(8,128)(2,1)S(1)} %get-tuple-element.36.expanded_ref, bf16[8,64,128]{2,1,0:T(8,128)(2,1)S(1)} %all_to_all.53.parts_ref, bf16[64,128]{1,0:T(8,128)(2,1)S(1)} %get-tuple-element.53.f0_ref, ...), custom_call_target="tpu_custom_call" | custom-call | tf_op jit(solution)/shard_map/final_currents/pallas_call | solution.py:374
  (2 shorter events, 0.0 us)
Async XLA Ops:
  2.5 8.7 %collective-permute-start.2 = (bf16[3,64,128]{2,1,0:T(8,128)(2,1)S(1)}, bf16[3,64,128]{2,1,0:T(8,128)(2,1)S(1)}, u32[]{:S(2)}, u32[]{:S(2)}) collective-permute-start(bf16[3,64,128]{2,1,0:T(8,128)(2,1)S(1)} %get-tuple-element.32.after_ref.own_ref), channel_id=1, source_target_pairs={{0,2},{1,3},{2,0},{3,1},{4,6},{5,7},{6,4},{7,5},{8,10},{9,11},{10,... | collective-permute-start | bytes 147464 | tf_op jit(solution)/shard_map/ppermute | solution.py:97
  5.6 5.5 %collective-permute-start.1 = (bf16[3,64,128]{2,1,0:T(8,128)(2,1)S(1)}, bf16[3,64,128]{2,1,0:T(8,128)(2,1)S(1)}, u32[]{:S(2)}, u32[]{:S(2)}) collective-permute-start(bf16[3,64,128]{2,1,0:T(8,128)(2,1)S(1)} %get-tuple-element.32.after_ref.own_ref), channel_id=1, source_target_pairs={{0,3},{1,2},{2,1},{3,0},{4,7},{5,6},{6,5},{7,4},{8,11},{9,10},{10,... | collective-permute-start | bytes 147464 | tf_op jit(solution)/shard_map/ppermute | solution.py:97
  6.8 4.4 %collective-permute-start = (bf16[3,64,128]{2,1,0:T(8,128)(2,1)S(1)}, bf16[3,64,128]{2,1,0:T(8,128)(2,1)S(1)}, u32[]{:S(2)}, u32[]{:S(2)}) collective-permute-start(bf16[3,64,128]{2,1,0:T(8,128)(2,1)S(1)} %get-tuple-element.32.after_ref.own_ref), channel_id=1, source_target_pairs={{0,1},{1,0},{2,3},{3,2},{4,5},{5,4},{6,7},{7,6},{8,9},{9,8},{10,11... | collective-permute-start | bytes 147464 | tf_op jit(solution)/shard_map/ppermute | solution.py:97
  6.8 11.8 %slice-start = ((s8[9437184]{0:T(1024)(128)(4,1)}), s8[4194304]{0:T(1024)(128)(4,1)S(1)}, s32[]{:S(2)}) async-start(s8[9437184]{0:T(1024)(128)(4,1)} %bitcast.6), calls=%async_computation.9 | async-start | bytes 8388608
  6.8 11.8 %slice-start.1 = ((s8[9437184]{0:T(1024)(128)(4,1)}), s8[4194304]{0:T(1024)(128)(4,1)S(1)}, s32[]{:S(2)}) async-start(s8[9437184]{0:T(1024)(128)(4,1)} %bitcast.6), calls=%async_computation.10 | async-start | bytes 8388608
  11.2 7.4 %slice-start.2 = ((s8[9437184]{0:T(1024)(128)(4,1)}), s8[1048576]{0:T(1024)(128)(4,1)S(1)}, s32[]{:S(2)}) async-start(s8[9437184]{0:T(1024)(128)(4,1)} %bitcast.6), calls=%async_computation.11 | async-start | bytes 2097152
  11.2 7.4 %copy-start = (bf16[2,64,1536]{2,1,0:T(8,128)(2,1)S(1)}, bf16[2,64,1536]{2,1,0:T(8,128)(2,1)}, u32[]{:S(2)}) copy-start(bf16[2,64,1536]{2,1,0:T(8,128)(2,1)} %proj_ref.3) | copy-start | bytes 1179652
  11.2 7.4 %copy-start.1 = (bf16[5,2,64,1536]{3,2,1,0:T(8,128)(2,1)S(1)}, bf16[5,2,64,1536]{3,2,1,0:T(8,128)(2,1)}, u32[]{:S(2)}) copy-start(bf16[5,2,64,1536]{3,2,1,0:T(8,128)(2,1)} %incident_ref.1) | copy-start | bytes 5898244
  11.2 7.4 %copy-start.2 = (bf16[2,64,1536]{2,1,0:T(8,128)(2,1)S(1)}, bf16[2,64,1536]{2,1,0:T(8,128)(2,1)}, u32[]{:S(2)}) copy-start(bf16[2,64,1536]{2,1,0:T(8,128)(2,1)} %expand_ref.1) | copy-start | bytes 1179652
  11.3 12.5 %collective-permute-start.5 = (bf16[4,3,64,128]{3,2,1,0:T(8,128)(2,1)S(1)}, bf16[4,3,64,128]{3,2,1,0:T(8,128)(2,1)S(1)}, u32[]{:S(2)}, u32[]{:S(2)}) collective-permute-start(bf16[4,3,64,128]{3,2,1,0:T(8,128)(2,1)S(1)} %order_x.1.after_ref.own_ref), channel_id=1, source_target_pairs={{0,8},{1,9},{2,10},{3,11},{4,12},{5,13},{6,14},{7,15},{8,0},{9,1},... | collective-permute-start | bytes 589832 | tf_op jit(solution)/shard_map/ppermute | solution.py:97
  14.5 9.2 %collective-permute-start.4 = (bf16[4,3,64,128]{3,2,1,0:T(8,128)(2,1)S(1)}, bf16[4,3,64,128]{3,2,1,0:T(8,128)(2,1)S(1)}, u32[]{:S(2)}, u32[]{:S(2)}) collective-permute-start(bf16[4,3,64,128]{3,2,1,0:T(8,128)(2,1)S(1)} %order_x.1.after_ref.own_ref), channel_id=1, source_target_pairs={{0,12},{1,13},{2,14},{3,15},{4,8},{5,9},{6,10},{7,11},{8,4},{9,5},... | collective-permute-start | bytes 589832 | tf_op jit(solution)/shard_map/ppermute | solution.py:97
  15.6 8.2 %collective-permute-start.3 = (bf16[4,3,64,128]{3,2,1,0:T(8,128)(2,1)S(1)}, bf16[4,3,64,128]{3,2,1,0:T(8,128)(2,1)S(1)}, u32[]{:S(2)}, u32[]{:S(2)}) collective-permute-start(bf16[4,3,64,128]{3,2,1,0:T(8,128)(2,1)S(1)} %order_x.1.after_ref.own_ref), channel_id=1, source_target_pairs={{0,4},{1,5},{2,6},{3,7},{4,0},{5,1},{6,2},{7,3},{8,12},{9,13},{10,... | collective-permute-start | bytes 589832 | tf_op jit(solution)/shard_map/ppermute | solution.py:97
